TPU v7x, 32 devices: a whole 2x2x4 slice. The times are simulated.
32 devices in a mesh: gx: 8 (over y, x, core), gy: 4 (over z).
Axes of the slice: x: 2, y: 2, z: 4, core: 2. Of those that a mesh axis runs over, the one named last changes fastest.
Arguments:
- features: bfloat16 [8, 4, 4, 6144], P('gx', 'gy'), may hold values from -6 to 6
- cotangent: bfloat16 [8, 4, 4, 6144], P('gx', 'gy'), may hold values from -6 to 6
- brick_slot: int32 [8, 4, 2, 2, 2], P('gx', 'gy'), may hold values from 0 to 4, as said below
- weight_one: bfloat16 [27, 96, 96], replicated, may hold values from -0.125 to 0.125
- weight_two: bfloat16 [27, 96, 96], replicated, may hold values from -0.125 to 0.125
- gain: float32 [96], replicated, may hold values from 0.1 to 1.9
- bias: float32 [96], replicated, may hold values from -0.5 to 0.5
Outputs:
- out: bfloat16 [8, 4, 4, 6144], P('gx', 'gy')
- grad_features: bfloat16 [8, 4, 4, 6144], P('gx', 'gy')
- grad_weight_one: float32 [27, 96, 96], replicated
- grad_weight_two: float32 [27, 96, 96], replicated
- grad_gain: float32 [96], replicated
- grad_bias: float32 [96], replicated
Inputs may be any that keep to these rules, and one draw needn't show every extreme that they name: `brick_slot`: on each slab the values below 4 are the slots 0 to n - 1, each in exactly one cell, for some n from 2 to 4; all other cells hold 4. At least one slab has n = 4.
All inputs are finite; a program needn't handle non-finite values.
Results may differ from a plain program's by a relative error of at most 0.003.
Values may be sent and summed in bfloat16 or wider, within the bound.
A program may use at most 64 MiB of HBM per device.

v0:
```python
import math

import jax
import jax.numpy as jnp
from jax import lax
from jax.sharding import PartitionSpec as P


def with_halo(block, sides, width):
    for axis, dim in sides:
        count = lax.axis_size(axis)
        forward = [(i, i + 1) for i in range(count - 1)]
        backward = [(target, source) for source, target in forward]
        low = lax.ppermute(
            lax.slice_in_dim(block, block.shape[dim] - width, None, axis=dim), axis, forward
        )
        high = lax.ppermute(lax.slice_in_dim(block, 0, width, axis=dim), axis, backward)
        block = jnp.concatenate([low, block, high], axis=dim)
    return block


def brick_layout(slot_cells, count_slots, cells_side, column):
    total_cells = slot_cells.shape[0]
    cell_ids = (
        jnp.zeros((count_slots + 1,), jnp.int32)
        .at[slot_cells]
        .set(jnp.arange(total_cells, dtype=jnp.int32))[:count_slots]
    )
    filled = jnp.sum((slot_cells < count_slots).astype(jnp.int32))
    live = (jnp.arange(count_slots, dtype=jnp.int32) < filled).astype(jnp.float32)
    cell_x = cell_ids // (cells_side * column)
    cell_y = cell_ids // column % cells_side
    cell_z = cell_ids % column
    return ((cell_x, cell_y, cell_z), live)


def assemble(ext_flat, cells, span_y, span_z):
    pieces_at = {-1: slice(3, 4), 0: slice(0, 4), 1: slice(0, 1)}
    planes = []
    for along_x in (-1, 0, 1):
        lines = []
        for along_y in (-1, 0, 1):
            blocks = []
            for along_z in (-1, 0, 1):
                rows_index = (
                    ((cells[0] + 1 + along_x) * span_y + cells[1] + 1 + along_y) * span_z
                    + cells[2]
                    + 1
                    + along_z
                )
                whole_bricks = jnp.take(ext_flat, rows_index, axis=0)
                blocks.append(
                    whole_bricks[:, pieces_at[along_x], pieces_at[along_y], pieces_at[along_z], :]
                )
            lines.append(jnp.concatenate(blocks, axis=3))
        planes.append(jnp.concatenate(lines, axis=2))
    return jnp.concatenate(planes, axis=1)


def plane_windows(padded, along_x):
    channels = padded.shape[-1]
    windows = []
    for along_y in (-1, 0, 1):
        for along_z in (-1, 0, 1):
            window = padded[
                :,
                1 + along_x : 5 + along_x,
                1 + along_y : 5 + along_y,
                1 + along_z : 5 + along_z,
                :,
            ]
            windows.append(window.reshape(-1, channels))
    return jnp.stack(windows, axis=0)


def conv_taps(padded, kernel):
    channels = kernel.shape[1]
    total = None
    for along_x in (-1, 0, 1):
        first_tap = 9 * (along_x + 1)
        stacked = plane_windows(padded, along_x)
        term = jnp.einsum(
            "trc,tcd->rd",
            stacked,
            kernel[first_tap : first_tap + 9],
            preferred_element_type=jnp.float32,
        )
        total = term if total is None else total + term
    return total.reshape(padded.shape[0], 4, 4, 4, channels)


def weight_taps(padded, grads):
    channels = grads.shape[-1]
    flat_grads = grads.reshape(-1, channels)
    results = []
    for along_x in (-1, 0, 1):
        stacked = plane_windows(padded, along_x)
        results.append(
            jnp.einsum("trc,rd->tcd", stacked, flat_grads, preferred_element_type=jnp.float32)
        )
    return jnp.concatenate(results, axis=0)


def flipped(kernel):
    return jnp.transpose(jnp.flip(kernel, 0), (0, 2, 1))


def halo_grid(dense_grid):
    cells_side = dense_grid.shape[0]
    column = dense_grid.shape[2]
    channels = dense_grid.shape[-1]
    voxels = dense_grid.transpose(0, 3, 1, 4, 2, 5, 6).reshape(
        cells_side * 4, cells_side * 4, column, 4, channels
    )
    bordered = with_halo(voxels, (("gx", 0), ("gy", 1)), 1)
    widened = jnp.pad(bordered, ((3, 3), (3, 3), (0, 0), (0, 0), (0, 0)))
    widened = widened.reshape(cells_side + 2, 4, cells_side + 2, 4, column, 4, channels)
    return widened.transpose(0, 2, 4, 1, 3, 5, 6)


def body(features, cotangent, brick_slot, weight_one, weight_two, gain, bias):
    count_slots = features.shape[2]
    channels = gain.shape[0]
    cells_side = brick_slot.shape[2]
    column = brick_slot.shape[4]
    slot_cells = brick_slot.reshape(-1)
    cells, live = brick_layout(slot_cells, count_slots, cells_side, column)
    live_five = live[:, None, None, None, None]
    inputs = features.reshape(count_slots, 4, 4, 4, channels)
    upstream = cotangent.reshape(count_slots, 4, 4, 4, channels)

    def padded_field(values):
        source_rows = jnp.concatenate(
            [values, jnp.zeros((1,) + values.shape[1:], values.dtype)], axis=0
        )
        dense_grid = jnp.take(source_rows, slot_cells, axis=0).reshape(
            (cells_side, cells_side, column) + values.shape[1:]
        )
        extended = halo_grid(dense_grid)
        blank = jnp.zeros(
            (extended.shape[0], extended.shape[1], 1) + extended.shape[3:], extended.dtype
        )
        extended = jnp.concatenate([blank, extended, blank], axis=2)
        ext_flat = extended.reshape((-1,) + extended.shape[3:])
        return assemble(ext_flat, cells, extended.shape[1], extended.shape[2])

    padded_inputs = padded_field(inputs)
    first_conv = conv_taps(padded_inputs, weight_one) * live_five
    pre = first_conv * gain + bias
    hidden = (jax.nn.silu(pre) * live_five).astype(jnp.bfloat16)
    padded_hidden = padded_field(hidden)
    out = (
        (inputs.astype(jnp.float32) + conv_taps(padded_hidden, weight_two) * live_five) * live_five
    ).astype(jnp.bfloat16)
    masked_cotangent = (upstream.astype(jnp.float32) * live_five).astype(jnp.bfloat16)
    grad_two_local = weight_taps(padded_hidden, masked_cotangent)
    back_hidden = conv_taps(padded_field(masked_cotangent), flipped(weight_two)) * live_five
    sigmoid = jax.nn.sigmoid(pre)
    back_pre = back_hidden * (sigmoid * (1.0 + pre * (1.0 - sigmoid)))
    gain_local = jnp.sum(back_pre * first_conv, axis=(0, 1, 2, 3))
    bias_local = jnp.sum(back_pre, axis=(0, 1, 2, 3))
    back_conv = (back_pre * gain).astype(jnp.bfloat16)
    grad_one_local = weight_taps(padded_inputs, back_conv)
    back_inputs = conv_taps(padded_field(back_conv), flipped(weight_one)) * live_five
    grad_features = ((upstream.astype(jnp.float32) + back_inputs) * live_five).astype(jnp.bfloat16)
    grad_one_total, grad_two_total, gain_total, bias_total = lax.psum(
        (grad_one_local, grad_two_local, gain_local, bias_local), ("gx", "gy")
    )
    slabs_all = lax.axis_size("gx") * lax.axis_size("gy")
    scale = 1.0 / math.sqrt(slabs_all * count_slots * 64)
    return (
        out.reshape(features.shape),
        grad_features.reshape(features.shape),
        grad_one_total * scale,
        grad_two_total * scale,
        gain_total * scale,
        bias_total * scale,
    )


def solution(mesh):
    in_specs = (
        P("gx", "gy", None, None),
        P("gx", "gy", None, None),
        P("gx", "gy", None, None, None),
        P(),
        P(),
        P(),
        P(),
    )
    out_specs = (P("gx", "gy", None, None), P("gx", "gy", None, None), P(), P(), P(), P())
    return jax.shard_map(body, mesh=mesh, in_specs=in_specs, out_specs=out_specs, check_vma=False)
```

profile of v0, /device:TPU:0, one launch (start us, length us, event | category | flops | bytes accessed | tf_op | source)
XLA Modules:
  0.0 564.3 jit_solution(4519285126870118928)
XLA Ops:
  15.1 1.4 collective-permute-start.9
  16.6 3.0 collective-permute-start.8
  21.1 5.1 collective-permute-start
  35.6 4.5 collective-permute-start.10
  41.5 4.5 collective-permute-start.2
  49.3 3.5 pad_maximum_fusion.1
  95.9 1.5 gather_fusion.66
  97.3 1.5 gather_fusion.10
  125.3 1.4 broadcast_select_fusion.17
  126.7 1.4 slice_select_fusion.4
  128.2 1.4 broadcast_select_fusion.21
  129.6 1.4 broadcast_select_fusion.61
  130.9 1.4 slice_select_fusion.21
  140.8 1.4 broadcast_select_fusion.37
  152.1 1.6 copy.648
  154.4 1.6 copy.650
  158.1 1.6 copy.653
  171.9 1.4 slice_select_fusion.22
  177.2 1.4 broadcast_select_fusion.77
  189.2 1.6 copy.519
  190.7 1.6 copy.520
  201.1 3.0 collective-permute-start.12
  205.5 4.3 collective-permute-start.4
  209.8 44.1 %all-reduce.8 = (f32[96]{0:T(128)S(1)}, f32[96]{0:T(128)S(1)}) all-reduce(f32[96]{0:T(128)S(1)} %get-tuple-element.9, f32[96]{0:T(128)S(1)} %get-tuple-element.8), channel_id=1, replica_groups=mesh['gx'=8,'gy'=4] {'gx','gy'}, use_global_device_ids=true, to_apply=%region_5.8 | all-reduce | flops 192 | bytes 1536 | tf_op jit(solution)/shard_map/psum | solution.py:166
  257.5 4.5 collective-permute-start.14
  263.4 4.5 collective-permute-start.6
  270.6 4.5 pad_maximum_fusion
  278.6 2.0 copy.560
  300.2 1.4 gather_fusion.47
  314.2 1.4 gather_fusion.40
  319.6 1.4 gather_fusion.38
  321.0 1.5 gather_fusion.93
  322.5 1.5 gather_fusion.37
  328.0 1.4 gather_fusion.35
  329.4 1.4 gather_fusion.90
  342.9 1.4 gather_fusion.85
  374.6 1.6 copy.707
  387.6 1.4 broadcast_select_fusion.68
  390.4 1.4 broadcast_select_fusion.72
  391.7 1.4 broadcast_select_fusion.40
  394.0 1.4 broadcast_select_fusion.44
  395.4 1.5 broadcast_select_fusion.76
  396.9 1.4 slice_select_fusion.19
  402.4 1.6 copy.696
  403.9 1.6 copy.697
  405.5 1.5 copy.698
  417.3 136.2 %all-reduce.12.cloned.1.call-done = (f32[27,96,96]{2,1,0:T(8,128)}, f32[27,96,96]{2,1,0:T(8,128)}) async-done(((f32[27,96,96]{2,1,0:T(8,128)}, f32[27,96,96]{2,1,0:T(8,128)}), (f32[27,96,96]{2,1,0:T(8,128)}, f32[27,96,96]{2,1,0:T(8,128)})) %all-reduce.12.cloned.1.call-update) | async-done | bytes 1990672 | tf_op jit(solution)/shard_map/psum | solution.py:166
  553.5 2.6 broadcast_multiply_fusion.1
  (813 shorter events, 270.6 us)
Async XLA Ops:
  7.2 546.3 %all-reduce.12.cloned.1.call-start = ((), (), s32[]{:S(2)}) async-start(), calls=%async_computation | async-start | bytes 5308416 | tf_op jit(solution)/shard_map/psum | solution.py:166
  13.5 106.5 %copy-start.63 = (s32[1024]{0:T(1024)}, s32[1024]{0:T(1024)S(1)}, u32[]{:S(2)}) copy-start(s32[1024]{0:T(1024)S(1)} %get-tuple-element.393) | copy-start | bytes 12292
  15.1 19.1 %collective-permute-start.9 = (bf16[1,8,2,4,96]{4,1,3,2,0:T(8,128)(2,1)S(1)}, bf16[1,8,2,4,96]{4,1,3,2,0:T(8,128)(2,1)S(1)}, u32[]{:S(2)}, u32[]{:S(2)}) collective-permute-start(bf16[1,8,2,4,96]{4,1,3,2,0:T(8,128)(2,1)S(1)} %get-tuple-element.189), channel_id=1, source_target_pairs={{4,0},{8,4},{12,8},{16,12},{20,16},{24,20},{28,24},{5,1},{9,5},{13... | collective-permute-start | bytes 36872 | tf_op jit(solution)/shard_map/ppermute | solution.py:17
  16.6 17.6 %collective-permute-start.8 = (bf16[1,8,2,4,96]{4,1,3,2,0:T(8,128)(2,1)S(1)}, bf16[1,8,2,4,96]{4,1,3,2,0:T(8,128)(2,1)S(1)}, u32[]{:S(2)}, u32[]{:S(2)}) collective-permute-start(bf16[1,8,2,4,96]{4,1,3,2,0:T(8,128)(2,1)S(1)} %get-tuple-element.188), channel_id=1, source_target_pairs={{0,4},{4,8},{8,12},{12,16},{16,20},{20,24},{24,28},{1,5},{5,9},{9,... | collective-permute-start | bytes 36872 | tf_op jit(solution)/shard_map/ppermute | solution.py:14
  19.8 20.3 %collective-permute-start.1 = (bf16[1,8,2,4,96]{4,1,3,2,0:T(8,128)(2,1)S(1)}, bf16[1,8,2,4,96]{4,1,3,2,0:T(8,128)(2,1)S(1)}, u32[]{:S(2)}, u32[]{:S(2)}) collective-permute-start(bf16[1,8,2,4,96]{4,1,3,2,0:T(8,128)(2,1)S(1)} %get-tuple-element.197), channel_id=1, source_target_pairs={{4,0},{8,4},{12,8},{16,12},{20,16},{24,20},{28,24},{5,1},{9,5},{13... | collective-permute-start | bytes 36872 | tf_op jit(solution)/shard_map/ppermute | solution.py:17
  21.1 19.1 %collective-permute-start = (bf16[1,8,2,4,96]{4,1,3,2,0:T(8,128)(2,1)S(1)}, bf16[1,8,2,4,96]{4,1,3,2,0:T(8,128)(2,1)S(1)}, u32[]{:S(2)}, u32[]{:S(2)}) collective-permute-start(bf16[1,8,2,4,96]{4,1,3,2,0:T(8,128)(2,1)S(1)} %get-tuple-element.196), channel_id=1, source_target_pairs={{0,4},{4,8},{8,12},{12,16},{16,20},{20,24},{24,28},{1,5},{5,9},{9,... | collective-permute-start | bytes 36872 | tf_op jit(solution)/shard_map/ppermute | solution.py:14
  26.9 36.2 %copy-start.65 = (s32[1024]{0:T(1024)}, s32[1024]{0:T(1024)S(1)}, u32[]{:S(2)}) copy-start(s32[1024]{0:T(1024)S(1)} %pad_clamp_fusion.3) | copy-start | bytes 12292
  26.9 38.6 %copy-start.64 = (s32[1024]{0:T(1024)}, s32[1024]{0:T(1024)S(1)}, u32[]{:S(2)}) copy-start(s32[1024]{0:T(1024)S(1)} %pad_clamp_fusion.4) | copy-start | bytes 12292
  27.5 42.9 %copy-start.73 = (s32[1024]{0:T(1024)}, s32[1024]{0:T(1024)S(1)}, u32[]{:S(2)}) copy-start(s32[1024]{0:T(1024)S(1)} %pad_clamp_fusion.6) | copy-start | bytes 12292
  27.6 45.3 %copy-start.72 = (s32[1024]{0:T(1024)}, s32[1024]{0:T(1024)S(1)}, u32[]{:S(2)}) copy-start(s32[1024]{0:T(1024)S(1)} %pad_clamp_fusion.7) | copy-start | bytes 12292
  27.6 50.2 %copy-start.67 = (s32[1024]{0:T(1024)}, s32[1024]{0:T(1024)S(1)}, u32[]{:S(2)}) copy-start(s32[1024]{0:T(1024)S(1)} %pad_clamp_fusion.9) | copy-start | bytes 12292
  27.6 52.7 %copy-start.66 = (s32[1024]{0:T(1024)}, s32[1024]{0:T(1024)S(1)}, u32[]{:S(2)}) copy-start(s32[1024]{0:T(1024)S(1)} %pad_clamp_fusion.10) | copy-start | bytes 12292
  28.2 56.9 %copy-start.76 = (s32[1024]{0:T(1024)}, s32[1024]{0:T(1024)S(1)}, u32[]{:S(2)}) copy-start(s32[1024]{0:T(1024)S(1)} %pad_clamp_fusion.12) | copy-start | bytes 12292
  28.3 58.7 %copy-start.75 = (s32[1024]{0:T(1024)}, s32[1024]{0:T(1024)S(1)}, u32[]{:S(2)}) copy-start(s32[1024]{0:T(1024)S(1)} %pad_clamp_fusion.13) | copy-start | bytes 12292
  28.3 63.9 %copy-start.71 = (s32[1024]{0:T(1024)}, s32[1024]{0:T(1024)S(1)}, u32[]{:S(2)}) copy-start(s32[1024]{0:T(1024)S(1)} %pad_clamp_fusion.15) | copy-start | bytes 12292
  28.3 66.3 %copy-start.70 = (s32[1024]{0:T(1024)}, s32[1024]{0:T(1024)S(1)}, u32[]{:S(2)}) copy-start(s32[1024]{0:T(1024)S(1)} %pad_clamp_fusion.16) | copy-start | bytes 12292
  28.9 71.1 %copy-start.78 = (s32[1024]{0:T(1024)}, s32[1024]{0:T(1024)S(1)}, u32[]{:S(2)}) copy-start(s32[1024]{0:T(1024)S(1)} %pad_clamp_fusion.18) | copy-start | bytes 12292
  29.0 73.6 %copy-start.77 = (s32[1024]{0:T(1024)}, s32[1024]{0:T(1024)S(1)}, u32[]{:S(2)}) copy-start(s32[1024]{0:T(1024)S(1)} %pad_clamp_fusion.19) | copy-start | bytes 12292
  29.0 78.5 %copy-start.74 = (s32[1024]{0:T(1024)}, s32[1024]{0:T(1024)S(1)}, u32[]{:S(2)}) copy-start(s32[1024]{0:T(1024)S(1)} %pad_clamp_fusion.21) | copy-start | bytes 12292
  29.6 38.4 %copy-start.86 = (s32[1024]{0:T(1024)}, s32[1024]{0:T(1024)S(1)}, u32[]{:S(2)}) copy-start(s32[1024]{0:T(1024)S(1)} %get-tuple-element.364) | copy-start | bytes 12292
  29.6 45.8 %copy-start.85 = (s32[1024]{0:T(1024)}, s32[1024]{0:T(1024)S(1)}, u32[]{:S(2)}) copy-start(s32[1024]{0:T(1024)S(1)} %get-tuple-element.365) | copy-start | bytes 12292
  29.6 53.1 %copy-start.83 = (s32[1024]{0:T(1024)}, s32[1024]{0:T(1024)S(1)}, u32[]{:S(2)}) copy-start(s32[1024]{0:T(1024)S(1)} %get-tuple-element.366) | copy-start | bytes 12292
  30.2 74.8 %copy-start.82 = (s32[1024]{0:T(1024)}, s32[1024]{0:T(1024)S(1)}, u32[]{:S(2)}) copy-start(s32[1024]{0:T(1024)S(1)} %get-tuple-element.369) | copy-start | bytes 12292
  30.2 82.4 %copy-start.80 = (s32[1024]{0:T(1024)}, s32[1024]{0:T(1024)S(1)}, u32[]{:S(2)}) copy-start(s32[1024]{0:T(1024)S(1)} %get-tuple-element.370) | copy-start | bytes 12292
  30.3 84.9 %copy-start.81 = (s32[1024]{0:T(1024)}, s32[1024]{0:T(1024)S(1)}, u32[]{:S(2)}) copy-start(s32[1024]{0:T(1024)S(1)} %get-tuple-element.391) | copy-start | bytes 12292
  30.3 87.3 %copy-start.79 = (s32[1024]{0:T(1024)}, s32[1024]{0:T(1024)S(1)}, u32[]{:S(2)}) copy-start(s32[1024]{0:T(1024)S(1)} %get-tuple-element.392) | copy-start | bytes 12292
  34.3 11.8 %collective-permute-start.11 = (bf16[10,1,2,4,96]{4,1,3,2,0:T(2,128)(2,1)S(1)}, bf16[10,1,2,4,96]{4,1,3,2,0:T(2,128)(2,1)S(1)}, u32[]{:S(2)}, u32[]{:S(2)}) collective-permute-start(bf16[10,1,2,4,96]{4,1,3,2,0:T(2,128)(2,1)S(1)} %get-tuple-element.163), channel_id=1, source_target_pairs={{1,0},{2,1},{3,2},{5,4},{6,5},{7,6},{9,8},{10,9},{11,10},{13,12},{... | collective-permute-start | bytes 46088 | tf_op jit(solution)/shard_map/ppermute | solution.py:17
  35.6 10.5 %collective-permute-start.10 = (bf16[10,1,2,4,96]{4,1,3,2,0:T(2,128)(2,1)S(1)}, bf16[10,1,2,4,96]{4,1,3,2,0:T(2,128)(2,1)S(1)}, u32[]{:S(2)}, u32[]{:S(2)}) collective-permute-start(bf16[10,1,2,4,96]{4,1,3,2,0:T(2,128)(2,1)S(1)} %get-tuple-element.162), channel_id=1, source_target_pairs={{0,1},{1,2},{2,3},{4,5},{5,6},{6,7},{8,9},{9,10},{10,11},{12,13},{... | collective-permute-start | bytes 46088 | tf_op jit(solution)/shard_map/ppermute | solution.py:14
  40.2 6.8 %collective-permute-start.3 = (bf16[10,1,2,4,96]{4,1,3,2,0:T(2,128)(2,1)S(1)}, bf16[10,1,2,4,96]{4,1,3,2,0:T(2,128)(2,1)S(1)}, u32[]{:S(2)}, u32[]{:S(2)}) collective-permute-start(bf16[10,1,2,4,96]{4,1,3,2,0:T(2,128)(2,1)S(1)} %get-tuple-element.179), channel_id=1, source_target_pairs={{1,0},{2,1},{3,2},{5,4},{6,5},{7,6},{9,8},{10,9},{11,10},{13,12},{... | collective-permute-start | bytes 46088 | tf_op jit(solution)/shard_map/ppermute | solution.py:17
  41.5 6.4 %collective-permute-start.2 = (bf16[10,1,2,4,96]{4,1,3,2,0:T(2,128)(2,1)S(1)}, bf16[10,1,2,4,96]{4,1,3,2,0:T(2,128)(2,1)S(1)}, u32[]{:S(2)}, u32[]{:S(2)}) collective-permute-start(bf16[10,1,2,4,96]{4,1,3,2,0:T(2,128)(2,1)S(1)} %get-tuple-element.178), channel_id=1, source_target_pairs={{0,1},{1,2},{2,3},{4,5},{5,6},{6,7},{8,9},{9,10},{10,11},{12,13},{... | collective-permute-start | bytes 46088 | tf_op jit(solution)/shard_map/ppermute | solution.py:14
  98.8 34.8 %copy-start.117 = (pred[4]{0:T(512)(128)(4,1)S(1)}, pred[4]{0:T(512)(128)(4,1)}, u32[]{:S(2)}) copy-start(pred[4]{0:T(512)(128)(4,1)} %get-tuple-element.376) | copy-start | bytes 16
  98.8 36.5 %copy-start.113 = (pred[4]{0:T(512)(128)(4,1)S(1)}, pred[4]{0:T(512)(128)(4,1)}, u32[]{:S(2)}) copy-start(pred[4]{0:T(512)(128)(4,1)} %get-tuple-element.378) | copy-start | bytes 16
  105.0 34.1 %copy-start.112 = (pred[4]{0:T(512)(128)(4,1)S(1)}, pred[4]{0:T(512)(128)(4,1)}, u32[]{:S(2)}) copy-start(pred[4]{0:T(512)(128)(4,1)} %get-tuple-element.381) | copy-start | bytes 16
  105.0 35.0 %copy-start.111 = (pred[4]{0:T(512)(128)(4,1)S(1)}, pred[4]{0:T(512)(128)(4,1)}, u32[]{:S(2)}) copy-start(pred[4]{0:T(512)(128)(4,1)} %get-tuple-element.384) | copy-start | bytes 16
  105.0 35.8 %copy-start.110 = (pred[4]{0:T(512)(128)(4,1)S(1)}, pred[4]{0:T(512)(128)(4,1)}, u32[]{:S(2)}) copy-start(pred[4]{0:T(512)(128)(4,1)} %get-tuple-element.383) | copy-start | bytes 16
  199.8 56.3 %collective-permute-start.13 = (bf16[1,8,2,4,96]{4,1,3,2,0:T(8,128)(2,1)S(1)}, bf16[1,8,2,4,96]{4,1,3,2,0:T(8,128)(2,1)S(1)}, u32[]{:S(2)}, u32[]{:S(2)}) collective-permute-start(bf16[1,8,2,4,96]{4,1,3,2,0:T(8,128)(2,1)S(1)} %get-tuple-element.185), channel_id=1, source_target_pairs={{4,0},{8,4},{12,8},{16,12},{20,16},{24,20},{28,24},{5,1},{9,5},{13... | collective-permute-start | bytes 36872 | tf_op jit(solution)/shard_map/ppermute | solution.py:17
  201.1 55.0 %collective-permute-start.12 = (bf16[1,8,2,4,96]{4,1,3,2,0:T(8,128)(2,1)S(1)}, bf16[1,8,2,4,96]{4,1,3,2,0:T(8,128)(2,1)S(1)}, u32[]{:S(2)}, u32[]{:S(2)}) collective-permute-start(bf16[1,8,2,4,96]{4,1,3,2,0:T(8,128)(2,1)S(1)} %get-tuple-element.184), channel_id=1, source_target_pairs={{0,4},{4,8},{8,12},{12,16},{16,20},{20,24},{24,28},{1,5},{5,9},{9,... | collective-permute-start | bytes 36872 | tf_op jit(solution)/shard_map/ppermute | solution.py:14
  204.2 57.8 %collective-permute-start.5 = (bf16[1,8,2,4,96]{4,1,3,2,0:T(8,128)(2,1)S(1)}, bf16[1,8,2,4,96]{4,1,3,2,0:T(8,128)(2,1)S(1)}, u32[]{:S(2)}, u32[]{:S(2)}) collective-permute-start(bf16[1,8,2,4,96]{4,1,3,2,0:T(8,128)(2,1)S(1)} %get-tuple-element.193), channel_id=1, source_target_pairs={{4,0},{8,4},{12,8},{16,12},{20,16},{24,20},{28,24},{5,1},{9,5},{13... | collective-permute-start | bytes 36872 | tf_op jit(solution)/shard_map/ppermute | solution.py:17
  205.5 56.6 %collective-permute-start.4 = (bf16[1,8,2,4,96]{4,1,3,2,0:T(8,128)(2,1)S(1)}, bf16[1,8,2,4,96]{4,1,3,2,0:T(8,128)(2,1)S(1)}, u32[]{:S(2)}, u32[]{:S(2)}) collective-permute-start(bf16[1,8,2,4,96]{4,1,3,2,0:T(8,128)(2,1)S(1)} %get-tuple-element.192), channel_id=1, source_target_pairs={{0,4},{4,8},{8,12},{12,16},{16,20},{20,24},{24,28},{1,5},{5,9},{9,... | collective-permute-start | bytes 36872 | tf_op jit(solution)/shard_map/ppermute | solution.py:14
  256.2 11.8 %collective-permute-start.15 = (bf16[10,1,2,4,96]{4,1,3,2,0:T(2,128)(2,1)S(1)}, bf16[10,1,2,4,96]{4,1,3,2,0:T(2,128)(2,1)S(1)}, u32[]{:S(2)}, u32[]{:S(2)}) collective-permute-start(bf16[10,1,2,4,96]{4,1,3,2,0:T(2,128)(2,1)S(1)} %get-tuple-element.155), channel_id=1, source_target_pairs={{1,0},{2,1},{3,2},{5,4},{6,5},{7,6},{9,8},{10,9},{11,10},{13,12},{... | collective-permute-start | bytes 46088 | tf_op jit(solution)/shard_map/ppermute | solution.py:17
  257.5 10.5 %collective-permute-start.14 = (bf16[10,1,2,4,96]{4,1,3,2,0:T(2,128)(2,1)S(1)}, bf16[10,1,2,4,96]{4,1,3,2,0:T(2,128)(2,1)S(1)}, u32[]{:S(2)}, u32[]{:S(2)}) collective-permute-start(bf16[10,1,2,4,96]{4,1,3,2,0:T(2,128)(2,1)S(1)} %get-tuple-element.154), channel_id=1, source_target_pairs={{0,1},{1,2},{2,3},{4,5},{5,6},{6,7},{8,9},{9,10},{10,11},{12,13},{... | collective-permute-start | bytes 46088 | tf_op jit(solution)/shard_map/ppermute | solution.py:14
  262.1 6.8 %collective-permute-start.7 = (bf16[10,1,2,4,96]{4,1,3,2,0:T(2,128)(2,1)S(1)}, bf16[10,1,2,4,96]{4,1,3,2,0:T(2,128)(2,1)S(1)}, u32[]{:S(2)}, u32[]{:S(2)}) collective-permute-start(bf16[10,1,2,4,96]{4,1,3,2,0:T(2,128)(2,1)S(1)} %get-tuple-element.171), channel_id=1, source_target_pairs={{1,0},{2,1},{3,2},{5,4},{6,5},{7,6},{9,8},{10,9},{11,10},{13,12},{... | collective-permute-start | bytes 46088 | tf_op jit(solution)/shard_map/ppermute | solution.py:17
  263.4 6.2 %collective-permute-start.6 = (bf16[10,1,2,4,96]{4,1,3,2,0:T(2,128)(2,1)S(1)}, bf16[10,1,2,4,96]{4,1,3,2,0:T(2,128)(2,1)S(1)}, u32[]{:S(2)}, u32[]{:S(2)}) collective-permute-start(bf16[10,1,2,4,96]{4,1,3,2,0:T(2,128)(2,1)S(1)} %get-tuple-element.170), channel_id=1, source_target_pairs={{0,1},{1,2},{2,3},{4,5},{5,6},{6,7},{8,9},{9,10},{10,11},{12,13},{... | collective-permute-start | bytes 46088 | tf_op jit(solution)/shard_map/ppermute | solution.py:14
  319.6 32.4 %copy-start.132 = (pred[4]{0:T(512)(128)(4,1)S(1)}, pred[4]{0:T(512)(128)(4,1)}, u32[]{:S(2)}) copy-start(pred[4]{0:T(512)(128)(4,1)} %get-tuple-element.354) | copy-start | bytes 16
  319.6 33.2 %copy-start.118 = (pred[4]{0:T(512)(128)(4,1)S(1)}, pred[4]{0:T(512)(128)(4,1)}, u32[]{:S(2)}) copy-start(pred[4]{0:T(512)(128)(4,1)} %get-tuple-element.376) | copy-start | bytes 16
  321.0 32.7 %copy-start.115 = (pred[4]{0:T(512)(128)(4,1)S(1)}, pred[4]{0:T(512)(128)(4,1)}, u32[]{:S(2)}) copy-start(pred[4]{0:T(512)(128)(4,1)} %get-tuple-element.379) | copy-start | bytes 16
  321.0 32.8 %copy-start.114 = (pred[4]{0:T(512)(128)(4,1)S(1)}, pred[4]{0:T(512)(128)(4,1)}, u32[]{:S(2)}) copy-start(pred[4]{0:T(512)(128)(4,1)} %get-tuple-element.378) | copy-start | bytes 16
  321.0 33.6 %copy-start.119 = (pred[4]{0:T(512)(128)(4,1)S(1)}, pred[4]{0:T(512)(128)(4,1)}, u32[]{:S(2)}) copy-start(pred[4]{0:T(512)(128)(4,1)} %get-tuple-element.349) | copy-start | bytes 16
  (117 other events, 1144.3 us)
Sparse Core Ops, SparseCore 0:
  415.9 137.5 all-reduce.11
where the time goes:
time: 575 us; the launch traced here: 564 us
  local copies, waits for them, and re-layouts  227 us (39%)
  waiting for transfers between devices  138 us (24%)
  other arithmetic  86.4 us (15%)
  starting transfers between devices  44.1 us (8%)
  blocking collectives  44.1 us (8%)
  between operations  18.1 us (3%)
  matrix products  6.53 us (1%)
    psum x1, waiting for transfers between devices, body(): lax.psum((grad_one_local, grad_two_local, gain_local, bias_local), ('gx',...  136 us
    gather x108, local copies, waits for them, and re-layouts, assemble(): whole_bricks = jnp.take(ext_flat, rows_index, axis=0)  134 us
    select_n x56, other arithmetic, assemble(): whole_bricks = jnp.take(ext_flat, rows_index, axis=0)  55.8 us
    another operation x120, local copies, waits for them, and re-layouts, plane_windows(): return jnp.stack(windows, axis=0)  44.5 us
    psum x1, blocking collectives, body(): lax.psum((grad_one_local, grad_two_local, gain_local, bias_local), ('gx',...  44.1 us
    ppermute x8, starting transfers between devices, with_halo(): lax.ppermute(lax.slice_in_dim(block, block.shape[dim] - width, None, axis...  33.6 us
    unnamed x392, local copies, waits for them, and re-layouts  24.1 us
  transfers between devices with their start and end apart: 17, of which 3 were waited for; matrix products, arithmetic and copies ran while one was open for 2% of the time, Pallas kernels for 0%

commit v1 on v0

v1 whole, which is shorter than its diff:
```python
import functools
import math

import jax
import jax.numpy as jnp
from jax import lax
from jax.experimental import pallas as pl
from jax.experimental.pallas import tpu as pltpu
from jax.sharding import PartitionSpec as P

F32 = jnp.float32
BF16 = jnp.bfloat16
MESH = pl.DeviceIdType.MESH
LANES = 128
TAPS = 27
OFFSETS = (-1, 0, 1)
DIRECTIONS = tuple((i, j) for i in OFFSETS for j in OFFSETS if (i, j) != (0, 0))


def source_range(step):
    return pl.ds(1, 8) if step == 0 else pl.ds(8 if step > 0 else 1, 1)


def landing_range(step):
    return pl.ds(1, 8) if step == 0 else pl.ds(0 if step > 0 else 9, 1)


def bit_orders(size_x, size_y):
    bits_x = [("gx", 1 << i) for i in range(size_x.bit_length() - 1)]
    bits_y = [("gy", 1 << i) for i in range(size_y.bit_length() - 1)]
    first = bits_x + bits_y
    second = bits_x[:1] + bits_x[1:][::-1] + bits_y
    return first, second


def kernel(
    size_x, size_y, tiles, scale,
    slots, fields, w_one, w_two, gain_in, bias_in,
    out, grad_out, gw_one, gw_two, gg_out, gb_out,
    held, held_two, shifted, cols_a, cols_b, wm_one, wm_two, wt_one, wt_two, pad_rows,
    red_a, red_b, in_a, in_b, all_a, all_b,
    halo_send, halo_recv, sum_send, sum_recv,
):
    px, py = lax.axis_index("gx"), lax.axis_index("gy")
    orders = bit_orders(size_x, size_y)
    stages = len(orders[0])

    def exists(dx, dy):
        ok = None
        for pos, step, size in ((px, dx, size_x), (py, dy, size_y)):
            if step == 0:
                continue
            one = pos + step < size if step > 0 else pos >= 1
            ok = one if ok is None else jnp.logical_and(ok, one)
        return ok

    def at_step(dx, dy):
        return {"gx": px + dx, "gy": py + dy}

    def my_bit(axis, bit):
        return lax.rem((px if axis == "gx" else py) // bit, 2)

    def partner(axis, bit):
        move = (1 - 2 * my_bit(axis, bit)) * bit
        return at_step(move, 0) if axis == "gx" else at_step(0, move)

    held[...] = jnp.zeros_like(held)
    held_two[...] = jnp.zeros_like(held_two)

    barrier = pltpu.get_barrier_semaphore()
    greeted = jnp.int32(0)
    for dx, dy in DIRECTIONS:
        there = exists(dx, dy)
        greeted = greeted + jnp.where(there, 1, 0)

        @pl.when(there)
        def _(dx=dx, dy=dy):
            pl.semaphore_signal(barrier, inc=1, device_id=at_step(dx, dy), device_id_type=MESH)

    for axis, bit in orders[0]:
        pl.semaphore_signal(barrier, inc=1, device_id=partner(axis, bit), device_id_type=MESH)

    z_index = lax.broadcasted_iota(jnp.int32, (1, 8, LANES), 1)
    low_half = jnp.where(z_index < 4, 1.0, 0.0).astype(F32)
    high_half = 1.0 - low_half
    cell_slot = [slots[c] for c in range(8)]

    def picks(i, j, s):
        cell = (i * 2 + j) * 2
        lower = jnp.where(cell_slot[cell] == s, 1.0, 0.0).astype(F32)
        upper = jnp.where(cell_slot[cell + 1] == s, 1.0, 0.0).astype(F32)
        return lower * low_half + upper * high_half

    masks = {(i, j, s): picks(i, j, s) for i in range(2) for j in range(2) for s in range(4)}
    filled = {
        (i, j): masks[i, j, 0] + masks[i, j, 1] + masks[i, j, 2] + masks[i, j, 3]
        for i in range(2)
        for j in range(2)
    }
    for f in range(2):
        for i in range(2):
            for j in range(2):
                total = fields[f, 0] * masks[i, j, 0]
                for s in range(1, 4):
                    total = total + fields[f, s] * masks[i, j, s]
                held[f, 1 + 4 * i : 5 + 4 * i, 1 + 4 * j : 5 + 4 * j] = total.reshape(
                    4, 4, 8, LANES
                )

    pl.semaphore_wait(barrier, greeted + stages)

    def halo_copy(buf, phase, number):
        dx, dy = DIRECTIONS[number]
        return pltpu.make_async_remote_copy(
            src_ref=buf.at[:, source_range(dx), source_range(dy)],
            dst_ref=buf.at[:, landing_range(dx), landing_range(dy)],
            send_sem=halo_send.at[phase, number],
            recv_sem=halo_recv.at[phase, number],
            device_id=at_step(dx, dy),
            device_id_type=MESH,
        )

    def halo_start(buf, phase):
        for number, (dx, dy) in enumerate(DIRECTIONS):

            @pl.when(exists(dx, dy))
            def _(number=number):
                halo_copy(buf, phase, number).start()

    def halo_arrive(buf, phase):
        for number, (dx, dy) in enumerate(DIRECTIONS):

            @pl.when(exists(-dx, -dy))
            def _(number=number):
                halo_copy(buf, phase, number).wait_recv()

    def halo_sent(buf, phase):
        for number, (dx, dy) in enumerate(DIRECTIONS):

            @pl.when(exists(dx, dy))
            def _(number=number):
                halo_copy(buf, phase, number).wait_send()

    halo_start(held, 0)

    for w_in, wide, turned in ((w_one, wm_one, wt_one), (w_two, wm_two, wt_two)):
        wide[...] = jnp.zeros_like(wide)
        for t in range(TAPS):
            wide[t * LANES : t * LANES + 96, 0:96] = w_in[t]
        for t in range(TAPS):
            flip = (TAPS - 1 - t) * LANES
            turned[t * LANES : (t + 1) * LANES, :] = (
                wide[flip : flip + LANES, :].astype(F32).T.astype(BF16)
            )
    pad_rows[...] = jnp.zeros_like(pad_rows)
    pad_rows[0:1, 0:96] = gain_in[...]
    pad_rows[1:2, 0:96] = bias_in[...]
    gain = pad_rows[0:1, :]
    bias = pad_rows[1:2, :]
    red_a[...] = jnp.zeros_like(red_a)
    red_b[...] = jnp.zeros_like(red_b)

    def columns(buf, f, cols):
        values = buf[f].reshape(100, 8, LANES)
        shifted[1] = values.reshape(10, 10, 8, LANES)
        shifted[0] = jnp.where(z_index == 0, 0.0, pltpu.roll(values, 1, 1)).reshape(
            10, 10, 8, LANES
        )
        shifted[2] = jnp.where(z_index == 7, 0.0, pltpu.roll(values, 7, 1)).reshape(
            10, 10, 8, LANES
        )
        for t in range(TAPS):
            a, b, c = t // 9, t // 3 % 3, t % 3
            cols[:, t * LANES : (t + 1) * LANES] = (
                shifted[c, a : a + 8, b : b + 8].reshape(512, LANES).astype(BF16)
            )

    def dense_mask():
        rows = []
        for i in range(2):
            line = jnp.concatenate(
                [jnp.broadcast_to(filled[i, j], (4, 8, LANES)) for j in range(2)], axis=0
            )
            rows.append(jnp.broadcast_to(line[None], (4, 8, 8, LANES)))
        return jnp.concatenate(rows, axis=0).reshape(512, LANES)

    def interior(buf, f):
        return buf[f, 1:9, 1:9].reshape(512, LANES)

    def dot(lhs, rhs):
        return jnp.dot(lhs, rhs, preferred_element_type=F32)

    def weight_sums(left, cols, red):
        left_t = left.T.astype(BF16)[0:96]
        for t in range(TAPS):
            red[pl.ds((TAPS - 1 - t) * 12, 12)] = dot(
                left_t, cols[:, t * LANES : (t + 1) * LANES]
            ).reshape(12, 8, LANES)

    halo_arrive(held, 0)
    occupied = dense_mask()
    columns(held, 0, cols_a)
    first_conv = dot(cols_a[...], wm_one[...]) * occupied
    pre = first_conv * gain + bias
    sigmoid = 1.0 / (1.0 + jnp.exp(-pre))
    hidden = occupied * (pre * sigmoid)
    held_two[0, 1:9, 1:9] = hidden.reshape(8, 8, 8, LANES)
    columns(held, 1, cols_b)
    back_hidden = dot(cols_b[...], wt_two[...]) * occupied
    back_pre = back_hidden * (sigmoid * (1.0 + pre * (1.0 - sigmoid)))
    held_two[1, 1:9, 1:9] = (back_pre * gain).reshape(8, 8, 8, LANES)
    halo_start(held_two, 1)
    red_b[TAPS * 12, 0:1, :] = jnp.sum(back_pre * first_conv, axis=0, keepdims=True)
    red_b[TAPS * 12, 1:2, :] = jnp.sum(back_pre, axis=0, keepdims=True)

    reds, ins, alls = (red_a, red_b), (in_a, in_b), (all_a, all_b)
    offsets = ([jnp.int32(0)], [jnp.int32(0)])

    def half_of(stage):
        return tiles >> (stage + 1)

    def scatter_copy(which, stage):
        axis, bit = orders[which][stage]
        half = half_of(stage)
        give = offsets[which][stage] + (1 - my_bit(axis, bit)) * half
        return pltpu.make_async_remote_copy(
            src_ref=reds[which].at[pl.ds(give, half)],
            dst_ref=ins[which].at[pl.ds(tiles - 2 * half, half)],
            send_sem=sum_send.at[which, stage],
            recv_sem=sum_recv.at[which, stage],
            device_id=partner(axis, bit),
            device_id_type=MESH,
        )

    def gather_copy(which, stage):
        axis, bit = orders[which][stage]
        half = half_of(stage)
        keep = offsets[which][stage + 1]
        rows = alls[which].at[pl.ds(keep, half)]
        return pltpu.make_async_remote_copy(
            src_ref=rows,
            dst_ref=rows,
            send_sem=sum_send.at[which, 2 * stages - 1 - stage],
            recv_sem=sum_recv.at[which, 2 * stages - 1 - stage],
            device_id=partner(axis, bit),
            device_id_type=MESH,
        )

    def scatter_end(which, stage):
        axis, bit = orders[which][stage]
        half = half_of(stage)
        scatter_copy(which, stage).wait()
        keep = offsets[which][stage] + my_bit(axis, bit) * half
        offsets[which].append(keep)
        total = reds[which][pl.ds(keep, half)] + ins[which][pl.ds(tiles - 2 * half, half)]
        if stage == stages - 1:
            alls[which][pl.ds(keep, half)] = total * scale
        else:
            reds[which][pl.ds(keep, half)] = total

    def advance(which, step):
        if step > 0:
            if step <= stages:
                scatter_end(which, step - 1)
            else:
                gather_copy(which, 2 * stages - step).wait()
        if step < stages:
            scatter_copy(which, step).start()
        elif step < 2 * stages:
            gather_copy(which, 2 * stages - 1 - step).start()

    weight_sums(interior(held_two, 0), cols_b, red_a)
    advance(0, 0)
    halo_arrive(held_two, 1)
    columns(held_two, 1, cols_a)
    weight_sums(interior(held, 0), cols_a, red_b)
    advance(1, 0)
    advance(0, 1)

    def to_slots(dense, ref):
        dense = dense.reshape(8, 8, 8, LANES)
        for s in range(4):
            total = None
            for i in range(2):
                for j in range(2):
                    part = dense[4 * i : 4 * i + 4, 4 * j : 4 * j + 4].reshape(16, 8, LANES)
                    part = part * masks[i, j, s]
                    total = part if total is None else total + part
            ref[s] = total + pltpu.roll(total, 4, 1)

    to_slots(interior(held, 1) + dot(cols_a[...], wt_one[...]), grad_out)
    advance(1, 1)
    columns(held_two, 0, cols_b)
    advance(0, 2)
    to_slots(interior(held, 0) + dot(cols_b[...], wm_two[...]), out)
    for step in range(2, 2 * stages + 1):
        advance(1, step)
        if step < 2 * stages:
            advance(0, step + 1)

    for t in range(TAPS):
        rows = pl.ds(t * 12, 12)
        gw_two[t] = all_a[rows].reshape(96, LANES)[:, 0:96]
        gw_one[t] = all_b[rows].reshape(96, LANES)[:, 0:96]
    gg_out[...] = all_b[TAPS * 12, 0:1, 0:96]
    gb_out[...] = all_b[TAPS * 12, 1:2, 0:96]
    halo_sent(held, 0)
    halo_sent(held_two, 1)


def body(features, cotangent, brick_slot, weight_one, weight_two, gain, bias):
    count_slots = features.shape[2]
    channels = gain.shape[0]
    size_x, size_y = lax.axis_size("gx"), lax.axis_size("gy")
    devices = size_x * size_y
    scale = 1.0 / math.sqrt(devices * count_slots * 64)
    tiles = -(-(TAPS * 12 + 1) // devices) * devices
    stages = (devices).bit_length() - 1
    fields = jnp.stack([features, cotangent]).reshape(2, count_slots, 16, 4, channels)
    fields = jnp.concatenate([fields, fields], axis=3).astype(F32)
    fields = jnp.pad(fields, ((0, 0), (0, 0), (0, 0), (0, 0), (0, LANES - channels)))
    vmem = pl.BlockSpec(memory_space=pltpu.VMEM)
    smem = pl.BlockSpec(memory_space=pltpu.SMEM)
    slot_shape = jax.ShapeDtypeStruct((count_slots, 16, 8, LANES), F32)
    weight_shape = jax.ShapeDtypeStruct((TAPS, channels, channels), F32)
    row_shape = jax.ShapeDtypeStruct((1, channels), F32)
    out, grad_features, gw_one, gw_two, gg, gb = pl.pallas_call(
        functools.partial(kernel, size_x, size_y, tiles, scale),
        out_shape=(slot_shape, slot_shape, weight_shape, weight_shape, row_shape, row_shape),
        in_specs=[smem] + [vmem] * 5,
        out_specs=(vmem,) * 6,
        scratch_shapes=[
            pltpu.VMEM((2, 10, 10, 8, LANES), F32),
            pltpu.VMEM((2, 10, 10, 8, LANES), F32),
            pltpu.VMEM((3, 10, 10, 8, LANES), F32),
            pltpu.VMEM((512, TAPS * LANES), BF16),
            pltpu.VMEM((512, TAPS * LANES), BF16),
            pltpu.VMEM((TAPS * LANES, LANES), BF16),
            pltpu.VMEM((TAPS * LANES, LANES), BF16),
            pltpu.VMEM((TAPS * LANES, LANES), BF16),
            pltpu.VMEM((TAPS * LANES, LANES), BF16),
            pltpu.VMEM((8, LANES), F32),
            pltpu.VMEM((tiles, 8, LANES), F32),
            pltpu.VMEM((tiles, 8, LANES), F32),
            pltpu.VMEM((tiles, 8, LANES), F32),
            pltpu.VMEM((tiles, 8, LANES), F32),
            pltpu.VMEM((tiles, 8, LANES), F32),
            pltpu.VMEM((tiles, 8, LANES), F32),
            pltpu.SemaphoreType.DMA((2, 8)),
            pltpu.SemaphoreType.DMA((2, 8)),
            pltpu.SemaphoreType.DMA((2, 2 * stages)),
            pltpu.SemaphoreType.DMA((2, 2 * stages)),
        ],
        compiler_params=pltpu.CompilerParams(
            collective_id=0, has_side_effects=True, vmem_limit_bytes=48 * 1024 * 1024
        ),
    )(
        brick_slot.reshape(-1),
        fields,
        weight_one,
        weight_two,
        gain.reshape(1, channels),
        bias.reshape(1, channels),
    )

    def pack(values):
        return values[:, :, :4, :channels].astype(BF16).reshape(features.shape)

    return (
        pack(out),
        pack(grad_features),
        gw_one,
        gw_two,
        gg.reshape(channels),
        gb.reshape(channels),
    )


def solution(mesh):
    in_specs = (
        P("gx", "gy", None, None),
        P("gx", "gy", None, None),
        P("gx", "gy", None, None, None),
        P(),
        P(),
        P(),
        P(),
    )
    out_specs = (P("gx", "gy", None, None), P("gx", "gy", None, None), P(), P(), P(), P())
    return jax.shard_map(body, mesh=mesh, in_specs=in_specs, out_specs=out_specs, check_vma=False)
```

time: 575 us -> 79.1 us (0.14); the launches traced: 564 us -> 78.8 us
  local copies, waits for them, and re-layouts: 227 us -> 11.4 us
  waiting for transfers between devices: 138 us -> 0 us
  other arithmetic: 86.4 us -> 0.21 us
  Pallas kernels: 0 us -> 66.5 us
  blocking collectives: 44.1 us -> 0 us
  starting transfers between devices: 44.1 us -> 0 us
  between operations: 18.1 us -> 0.7 us
  matrix products: 6.53 us -> 0 us
    gather x112 -> x0, local copies, waits for them, and re-layouts: 137 us -> none  [the longest x108 134 us: assemble(): whole_bricks = jnp.take(ext_flat, rows_index, axis=0)]
    psum x1 -> x0, waiting for transfers between devices: 136 us -> none  [body(): lax.psum((grad_one_local, grad_two_local, gain_local, bias_local), ('gx',...]
    pallas_call x0 -> x1, Pallas kernels: none -> 66.5 us  [body(): pl.pallas_call(functools.partial(kernel, size_x, size_y, tiles, scale), o...]
    select_n x60 -> x0, other arithmetic: 56.2 us -> none  [the longest x56 55.8 us: assemble(): whole_bricks = jnp.take(ext_flat, rows_index, axis=0)]
    psum x1 -> x0, blocking collectives: 44.1 us -> none  [body(): lax.psum((grad_one_local, grad_two_local, gain_local, bias_local), ('gx',...]
    ppermute x16 -> x0, starting transfers between devices: 44.1 us -> none  [the longest x8 33.6 us: with_halo(): lax.ppermute(lax.slice_in_dim(block, block.shape[dim] - width, None, axis...]
    another operation x121 -> x2, local copies, waits for them, and re-layouts: 44.9 us -> 1.82 us  [body(): jnp.stack([features, cotangent]).reshape(2, count_slots, 16, 4, channels)]
    unnamed x392 -> x14, local copies, waits for them, and re-layouts: 24.1 us -> 6.24 us
  transfers between devices with their start and end apart: 17 -> 0, of which waited for: 3 -> 0; matrix products, arithmetic and copies ran while one was open for 2% -> 0% of each run, Pallas kernels for 0% -> 0%
where the time goes in v1:
time: 79.1 us; the launch traced here: 78.8 us
  Pallas kernels  66.5 us (84%)
  local copies, waits for them, and re-layouts  11.4 us (14%)
    pallas_call x1, Pallas kernels, body(): pl.pallas_call(functools.partial(kernel, size_x, size_y, tiles, scale), o...  66.5 us
    unnamed x14, local copies, waits for them, and re-layouts  6.24 us
    another operation x2, local copies, waits for them, and re-layouts, body(): jnp.stack([features, cotangent]).reshape(2, count_slots, 16, 4, channels)  1.82 us

profile of v1, /device:TPU:0, one launch (start us, length us, event | category | flops | bytes accessed | tf_op | source)
XLA Modules:
  0.0 78.8 jit_solution(11536590208652125285)
XLA Ops:
  0.6 0.0 copy-start
  0.6 0.8 %reshape.38.slots = s32[8]{0:T(128)S(1)} reshape(s32[1,1,2,2,2]{4,3,2,1,0:T(2,128)} %param.9) | data formatting | bytes 64 | tf_op jit(solution)/shard_map/reshape | solution.py:358
  1.5 0.9 %stack.9 = bf16[1,4,16,4,96]{4,3,2,1,0:T(4,128)(2,1)S(1)} reshape(bf16[1,1,4,6144]{3,2,1,0:T(4,128)(2,1)} %param.7) | data formatting | bytes 98304 | tf_op jit(solution)/shard_map/stack | solution.py:319
  2.4 0.9 %stack.10 = bf16[1,4,16,4,96]{4,3,2,1,0:T(4,128)(2,1)S(1)} reshape(bf16[1,1,4,6144]{3,2,1,0:T(4,128)(2,1)} %param.8) | data formatting | bytes 98304 | tf_op jit(solution)/shard_map/stack | solution.py:319
  3.3 0.2 fusion.6.fields
  3.5 0.0 copy-done
  3.5 0.0 copy-start.1
  3.5 1.1 %copy-done.1 = bf16[27,96,96]{2,1,0:T(8,128)(2,1)S(1)} copy-done((bf16[27,96,96]{2,1,0:T(8,128)(2,1)S(1)}, bf16[27,96,96]{2,1,0:T(8,128)(2,1)}, u32[]{:S(2)}) %copy-start.1) | copy-done | bytes 497688
  4.6 0.0 copy-start.3
  4.6 0.7 copy-done.3
  5.3 0.0 copy-start.4
  5.3 0.7 copy-done.4
  5.9 66.5 %shard_map.118 = (f32[4,16,8,128]{3,2,1,0:T(8,128)S(1)}, f32[4,16,8,128]{3,2,1,0:T(8,128)S(1)}, f32[27,96,96]{2,1,0:T(8,128)S(1)}, f32[27,96,96]{2,1,0:T(8,128)S...) custom-call(s32[8]{0:T(128)S(1)} %reshape.38.slots, f32[2,4,16,8,128]{4,3,2,1,0:T(8,128)S(1)} %fusion.6.fields, ...), custom_call_target="tpu_custom_call" | custom-call | tf_op jit(solution)/shard_map/pallas_call | solution.py:327
  72.4 0.0 copy-start.2
  72.4 0.7 copy-done.2
  73.2 0.8 reshape.41
  73.9 1.0 %slice.14 = bf16[4,16,4,96]{3,2,1,0:T(4,128)(2,1)S(1)} slice(f32[4,16,8,128]{3,2,1,0:T(8,128)} %copy-done.2), slice={[0:4], [0:16], [0:4], [0:96]} | slice | bytes 98304 | tf_op jit(solution)/shard_map/slice | solution.py:367
  74.9 0.8 reshape.42
  75.7 1.1 %copy.17 = f32[27,96,96]{2,1,0:T(8,128)} copy(f32[27,96,96]{2,1,0:T(8,128)S(1)} %get-tuple-element.26) | data formatting | bytes 1990656
  76.7 1.1 %copy.18 = f32[27,96,96]{2,1,0:T(8,128)} copy(f32[27,96,96]{2,1,0:T(8,128)S(1)} %get-tuple-element.27) | data formatting | bytes 1990656
  77.8 0.5 copy.19
  78.3 0.5 copy.20
  (1 shorter events, 0.0 us)
Async XLA Ops:
  0.6 2.9 %copy-start = (bf16[27,96,96]{2,1,0:T(8,128)(2,1)S(1)}, bf16[27,96,96]{2,1,0:T(8,128)(2,1)}, u32[]{:S(2)}) copy-start(bf16[27,96,96]{2,1,0:T(8,128)(2,1)} %w_one.1) | copy-start | bytes 1492996
  3.5 1.1 %copy-start.1 = (bf16[27,96,96]{2,1,0:T(8,128)(2,1)S(1)}, bf16[27,96,96]{2,1,0:T(8,128)(2,1)}, u32[]{:S(2)}) copy-start(bf16[27,96,96]{2,1,0:T(8,128)(2,1)} %w_two.1) | copy-start | bytes 1492996
  4.6 0.7 copy-start.3
  5.3 0.7 copy-start.4
  72.4 0.7 copy-start.2

commit v2 on v1

v2 whole, which is shorter than its diff:
```python
import functools
import math

import jax
import jax.numpy as jnp
from jax import lax
from jax.experimental import pallas as pl
from jax.experimental.pallas import tpu as pltpu
from jax.sharding import PartitionSpec as P

F32 = jnp.float32
BF16 = jnp.bfloat16
MESH = pl.DeviceIdType.MESH
LANES = 128
TAPS = 27
OFFSETS = (-1, 0, 1)
DIRECTIONS = tuple((i, j) for i in OFFSETS for j in OFFSETS if (i, j) != (0, 0))


def source_range(step):
    return pl.ds(1, 8) if step == 0 else pl.ds(8 if step > 0 else 1, 1)


def landing_range(step):
    return pl.ds(1, 8) if step == 0 else pl.ds(0 if step > 0 else 9, 1)


RIDERS = (1, 4, 7, 10, 13, 16)
HOSTS = tuple(t for t in range(TAPS) if t not in RIDERS)
BLOCKS = len(HOSTS)


def rider(block):
    return (RIDERS[block // 3], block % 3) if block < 3 * len(RIDERS) else None


def sum_groups(size_x, size_y):
    groups = [("gx", 1, 2), ("gx", 2, size_x // 2), ("gy", 1, size_y)]
    return [group for group in groups if group[2] > 1]


def kernel(
    size_x, size_y, tiles, scale,
    slots, fields, w_one, w_two, gain_in, bias_in,
    out, grad_out, gw_one, gw_two, gg_out, gb_out,
    held, held_two, shifted, cols_a, cols_b, wm_one, wm_two, wt_one, wt_two, pad_rows,
    raw, w_here, red_a, red_b, in_a, in_b, all_a, all_b,
    halo_send, halo_recv, sum_send, sum_recv, all_send, all_recv, w_sem,
):
    px, py = lax.axis_index("gx"), lax.axis_index("gy")
    groups = sum_groups(size_x, size_y)
    stages = len(groups)
    loads = [
        pltpu.make_async_copy(w_in, w_here.at[n], w_sem.at[n])
        for n, w_in in enumerate((w_one, w_two))
    ]
    for load in loads:
        load.start()

    def exists(dx, dy):
        ok = None
        for pos, step, size in ((px, dx, size_x), (py, dy, size_y)):
            if step == 0:
                continue
            one = pos + step < size if step > 0 else pos >= 1
            ok = one if ok is None else jnp.logical_and(ok, one)
        return ok

    def at_step(dx, dy):
        return {"gx": px + dx, "gy": py + dy}

    def rank_in(group):
        axis, stride, count = group
        return lax.rem((px if axis == "gx" else py) // stride, count)

    def member(group, rank):
        axis, stride, _ = group
        move = (rank - rank_in(group)) * stride
        return at_step(move, 0) if axis == "gx" else at_step(0, move)

    held[...] = jnp.zeros_like(held)
    held_two[...] = jnp.zeros_like(held_two)

    barrier = pltpu.get_barrier_semaphore()
    greeted = jnp.int32(0)
    for dx, dy in DIRECTIONS:
        there = exists(dx, dy)
        greeted = greeted + jnp.where(there, 1, 0)

        @pl.when(there)
        def _(dx=dx, dy=dy):
            pl.semaphore_signal(barrier, inc=1, device_id=at_step(dx, dy), device_id_type=MESH)

    for group in groups:
        for turn in range(1, group[2]):
            other = lax.rem(rank_in(group) + turn, group[2])
            pl.semaphore_signal(
                barrier, inc=1, device_id=member(group, other), device_id_type=MESH
            )

    z_index = lax.broadcasted_iota(jnp.int32, (1, 8, LANES), 1)
    lane_index = lax.broadcasted_iota(jnp.int32, (1, 8, LANES), 2)
    low_half = jnp.where(z_index < 4, 1.0, 0.0).astype(F32)
    high_half = 1.0 - low_half
    cell_slot = [slots[0, 0, c // 4, c // 2 % 2, c % 2] for c in range(8)]

    def picks(i, j, s):
        cell = (i * 2 + j) * 2
        lower = jnp.where(cell_slot[cell] == s, 1.0, 0.0).astype(F32)
        upper = jnp.where(cell_slot[cell + 1] == s, 1.0, 0.0).astype(F32)
        return lower * low_half + upper * high_half

    masks = {(i, j, s): picks(i, j, s) for i in range(2) for j in range(2) for s in range(4)}
    filled = {
        (i, j): masks[i, j, 0] + masks[i, j, 1] + masks[i, j, 2] + masks[i, j, 3]
        for i in range(2)
        for j in range(2)
    }
    for f in range(2):
        for i in range(2):
            for j in range(2):
                total = fields[f, 0] * masks[i, j, 0]
                for s in range(1, 4):
                    total = total + fields[f, s] * masks[i, j, s]
                held[f, 1 + 4 * i : 5 + 4 * i, 1 + 4 * j : 5 + 4 * j] = total.reshape(
                    4, 4, 8, LANES
                )

    pl.semaphore_wait(barrier, greeted + sum(group[2] - 1 for group in groups))

    def halo_copy(buf, phase, number):
        dx, dy = DIRECTIONS[number]
        return pltpu.make_async_remote_copy(
            src_ref=buf.at[:, source_range(dx), source_range(dy)],
            dst_ref=buf.at[:, landing_range(dx), landing_range(dy)],
            send_sem=halo_send.at[phase, number],
            recv_sem=halo_recv.at[phase, number],
            device_id=at_step(dx, dy),
            device_id_type=MESH,
        )

    def halo_start(buf, phase):
        for number, (dx, dy) in enumerate(DIRECTIONS):

            @pl.when(exists(dx, dy))
            def _(number=number):
                halo_copy(buf, phase, number).start()

    def halo_arrive(buf, phase):
        for number, (dx, dy) in enumerate(DIRECTIONS):

            @pl.when(exists(-dx, -dy))
            def _(number=number):
                halo_copy(buf, phase, number).wait_recv()

    def halo_sent(buf, phase):
        for number, (dx, dy) in enumerate(DIRECTIONS):

            @pl.when(exists(dx, dy))
            def _(number=number):
                halo_copy(buf, phase, number).wait_send()

    halo_start(held, 0)

    raw[...] = jnp.zeros_like(raw)
    for n, (wide, turned) in enumerate(((wm_one, wt_one), (wm_two, wt_two))):
        loads[n].wait()
        for t in range(TAPS):
            raw[t * LANES : t * LANES + 96, 0:96] = w_here[n, t]
        turns = {}
        for t in range(TAPS):
            flip = (TAPS - 1 - t) * LANES
            turns[t] = raw[flip : flip + LANES, :].astype(F32).T.astype(BF16)
        for block, t in enumerate(HOSTS):
            at = block * LANES
            wide[at : at + LANES, :] = raw[t * LANES : (t + 1) * LANES, :]
            turned[at : at + LANES, :] = turns[t]
            if rider(block):
                extra, third = rider(block)
                rows = extra * LANES + third * 32
                wide[at + 96 : at + LANES, :] = raw[rows : rows + 32, :]
                turned[at + 96 : at + LANES, :] = turns[extra][third * 32 : third * 32 + 32]
    pad_rows[...] = jnp.zeros_like(pad_rows)
    pad_rows[0:1, 0:96] = gain_in[...]
    pad_rows[1:2, 0:96] = bias_in[...]
    gain = pad_rows[0:1, :]
    bias = pad_rows[1:2, :]
    red_a[...] = jnp.zeros_like(red_a)
    red_b[...] = jnp.zeros_like(red_b)

    def columns(buf, f, cols):
        values = buf[f].reshape(100, 8, LANES)
        shifted[1] = values.reshape(10, 10, 8, LANES)
        shifted[0] = jnp.where(z_index == 0, 0.0, pltpu.roll(values, 1, 1)).reshape(
            10, 10, 8, LANES
        )
        shifted[2] = jnp.where(z_index == 7, 0.0, pltpu.roll(values, 7, 1)).reshape(
            10, 10, 8, LANES
        )
        for third in range(3):
            turned = pltpu.roll(values, 96 - 32 * third, 2)
            shifted[3 + third] = jnp.where(lane_index >= 96, turned, 0.0).reshape(
                10, 10, 8, LANES
            )

        def window(t, version):
            a, b = t // 9, t // 3 % 3
            return shifted[version, a : a + 8, b : b + 8].reshape(512, LANES)

        for block, t in enumerate(HOSTS):
            values = window(t, t % 3)
            if rider(block):
                values = values + window(rider(block)[0], 3 + rider(block)[1])
            cols[:, block * LANES : (block + 1) * LANES] = values.astype(BF16)

    def dense_mask():
        rows = []
        for i in range(2):
            line = jnp.concatenate(
                [jnp.broadcast_to(filled[i, j], (4, 8, LANES)) for j in range(2)], axis=0
            )
            rows.append(jnp.broadcast_to(line[None], (4, 8, 8, LANES)))
        return jnp.concatenate(rows, axis=0).reshape(512, LANES)

    def interior(buf, f):
        return buf[f, 1:9, 1:9].reshape(512, LANES)

    def dot(lhs, rhs):
        return jnp.dot(lhs, rhs, preferred_element_type=F32)

    def weight_sums(left, cols, red):
        left_t = left.T.astype(BF16)[0:96]
        for block in range(BLOCKS):
            red[pl.ds(block * 12, 12)] = dot(
                left_t, cols[:, block * LANES : (block + 1) * LANES]
            ).reshape(12, 8, LANES)

    halo_arrive(held, 0)
    occupied = dense_mask()
    columns(held, 0, cols_a)
    first_conv = dot(cols_a[...], wm_one[...]) * occupied
    pre = first_conv * gain + bias
    sigmoid = 1.0 / (1.0 + jnp.exp(-pre))
    hidden = occupied * (pre * sigmoid)
    held_two[0, 1:9, 1:9] = hidden.reshape(8, 8, 8, LANES)
    columns(held, 1, cols_b)
    back_hidden = dot(cols_b[...], wt_two[...]) * occupied
    back_pre = back_hidden * (sigmoid * (1.0 + pre * (1.0 - sigmoid)))
    held_two[1, 1:9, 1:9] = (back_pre * gain).reshape(8, 8, 8, LANES)
    halo_start(held_two, 1)
    red_b[BLOCKS * 12, 0:1, :] = jnp.sum(back_pre * first_conv, axis=0, keepdims=True)
    red_b[BLOCKS * 12, 1:2, :] = jnp.sum(back_pre, axis=0, keepdims=True)

    reds, ins, alls = (red_a, red_b), (in_a, in_b), (all_a, all_b)
    offsets = ([jnp.int32(0)], [jnp.int32(0)])
    pieces, landings, first_sem = [], [], []
    length, landing, sems = tiles, 0, 0
    for group in groups:
        length = length // group[2]
        pieces.append(length)
        landings.append(landing)
        first_sem.append(sems)
        landing += length * (group[2] - 1)
        sems += group[2] - 1

    def scatter_copies(which, stage):
        group, piece = groups[stage], pieces[stage]
        copies = []
        for turn in range(1, group[2]):
            other = lax.rem(rank_in(group) + turn, group[2])
            sem = first_sem[stage] + turn - 1
            copies.append(
                pltpu.make_async_remote_copy(
                    src_ref=reds[which].at[pl.ds(offsets[which][stage] + other * piece, piece)],
                    dst_ref=ins[which].at[pl.ds(landings[stage] + (turn - 1) * piece, piece)],
                    send_sem=sum_send.at[which, sem],
                    recv_sem=sum_recv.at[which, sem],
                    device_id=member(group, other),
                    device_id_type=MESH,
                )
            )
        return copies

    def gather_copies(which, stage):
        group, piece = groups[stage], pieces[stage]
        copies = []
        for turn in range(1, group[2]):
            other = lax.rem(rank_in(group) + turn, group[2])
            sem = first_sem[stage] + turn - 1
            rows = alls[which].at[pl.ds(offsets[which][stage + 1] // 2, piece // 2)]
            copies.append(
                pltpu.make_async_remote_copy(
                    src_ref=rows,
                    dst_ref=rows,
                    send_sem=all_send.at[which, sem],
                    recv_sem=all_recv.at[which, sem],
                    device_id=member(group, other),
                    device_id_type=MESH,
                )
            )
        return copies

    def scatter_end(which, stage):
        group, piece = groups[stage], pieces[stage]
        for copy in scatter_copies(which, stage):
            copy.wait()
        keep = offsets[which][stage] + rank_in(group) * piece
        offsets[which].append(keep)
        total = reds[which][pl.ds(keep, piece)]
        for turn in range(group[2] - 1):
            total = total + ins[which][pl.ds(landings[stage] + turn * piece, piece)]
        if stage == stages - 1:
            alls[which][pl.ds(keep // 2, piece // 2)] = (
                (total * scale).reshape(piece // 2, 16, LANES).astype(BF16)
            )
        else:
            reds[which][pl.ds(keep, piece)] = total

    def advance(which, step):
        if step > 2 * stages:
            return
        if step > 0:
            if step <= stages:
                scatter_end(which, step - 1)
            else:
                for copy in gather_copies(which, 2 * stages - step):
                    copy.wait()
        if step < stages:
            copies = scatter_copies(which, step)
        elif step < 2 * stages:
            copies = gather_copies(which, 2 * stages - 1 - step)
        else:
            copies = []
        for copy in copies:
            copy.start()

    weight_sums(interior(held_two, 0), cols_b, red_a)
    advance(0, 0)
    halo_arrive(held_two, 1)
    columns(held_two, 1, cols_a)
    weight_sums(interior(held, 0), cols_a, red_b)
    advance(1, 0)
    advance(0, 1)

    def to_slots(dense, ref):
        dense = dense.reshape(8, 8, 8, LANES)
        for s in range(4):
            total = None
            for i in range(2):
                for j in range(2):
                    part = dense[4 * i : 4 * i + 4, 4 * j : 4 * j + 4].reshape(16, 8, LANES)
                    part = part * masks[i, j, s]
                    total = part if total is None else total + part
            ref[s] = (total + pltpu.roll(total, 4, 1))[:, 0:4, 0:96]

    to_slots(interior(held, 1) + dot(cols_a[...], wt_one[...]), grad_out)
    advance(1, 1)
    columns(held_two, 0, cols_b)
    advance(0, 2)
    to_slots(interior(held, 0) + dot(cols_b[...], wm_two[...]), out)
    def unpack(summed, gw):
        for block, t in enumerate(HOSTS):
            values = summed[pl.ds(block * 6, 6)].astype(F32).reshape(96, LANES)
            gw[TAPS - 1 - t] = values[:, 0:96]
            if rider(block):
                extra, third = rider(block)
                lanes = slice(third * 32, third * 32 + 32)
                gw[TAPS - 1 - extra, :, lanes] = pltpu.roll(values, third * 32 + 32, 1)[:, lanes]

    for step in range(2, 2 * stages + 1):
        advance(1, step)
        advance(0, step + 1)
        if step + 1 == 2 * stages:
            unpack(all_a, gw_two)
    unpack(all_b, gw_one)
    last = all_b[BLOCKS * 6].astype(F32)
    gg_out[...] = last[0:1, 0:96]
    gb_out[...] = last[1:2, 0:96]
    halo_sent(held, 0)
    halo_sent(held_two, 1)


def body(features, cotangent, brick_slot, weight_one, weight_two, gain, bias):
    count_slots = features.shape[2]
    channels = gain.shape[0]
    size_x, size_y = lax.axis_size("gx"), lax.axis_size("gy")
    devices = size_x * size_y
    scale = 1.0 / math.sqrt(devices * count_slots * 64)
    tiles = -(-(BLOCKS * 12 + 1) // (2 * devices)) * 2 * devices
    copies = sum(group[2] - 1 for group in sum_groups(size_x, size_y))
    fields = jnp.stack([features, cotangent]).reshape(2, count_slots, 16, 4, channels)
    fields = jnp.concatenate([fields, fields], axis=3).astype(F32)
    fields = jnp.pad(fields, ((0, 0), (0, 0), (0, 0), (0, 0), (0, LANES - channels)))
    vmem = pl.BlockSpec(memory_space=pltpu.VMEM)
    smem = pl.BlockSpec(memory_space=pltpu.SMEM)
    hbm = pl.BlockSpec(memory_space=pltpu.HBM)
    slot_shape = jax.ShapeDtypeStruct((count_slots, 16, 4, channels), F32)
    weight_shape = jax.ShapeDtypeStruct((TAPS, channels, channels), F32)
    row_shape = jax.ShapeDtypeStruct((1, channels), F32)
    out, grad_features, gw_one, gw_two, gg, gb = pl.pallas_call(
        functools.partial(kernel, size_x, size_y, tiles, scale),
        out_shape=(slot_shape, slot_shape, weight_shape, weight_shape, row_shape, row_shape),
        in_specs=[smem, vmem, hbm, hbm, vmem, vmem],
        out_specs=(vmem,) * 6,
        scratch_shapes=[
            pltpu.VMEM((2, 10, 10, 8, LANES), F32),
            pltpu.VMEM((2, 10, 10, 8, LANES), F32),
            pltpu.VMEM((6, 10, 10, 8, LANES), F32),
            pltpu.VMEM((512, BLOCKS * LANES), BF16),
            pltpu.VMEM((512, BLOCKS * LANES), BF16),
            pltpu.VMEM((BLOCKS * LANES, LANES), BF16),
            pltpu.VMEM((BLOCKS * LANES, LANES), BF16),
            pltpu.VMEM((BLOCKS * LANES, LANES), BF16),
            pltpu.VMEM((BLOCKS * LANES, LANES), BF16),
            pltpu.VMEM((8, LANES), F32),
            pltpu.VMEM((TAPS * LANES, LANES), BF16),
            pltpu.VMEM((2, TAPS, channels, channels), BF16),
            pltpu.VMEM((tiles, 8, LANES), F32),
            pltpu.VMEM((tiles, 8, LANES), F32),
            pltpu.VMEM((tiles, 8, LANES), F32),
            pltpu.VMEM((tiles, 8, LANES), F32),
            pltpu.VMEM((tiles // 2, 16, LANES), BF16),
            pltpu.VMEM((tiles // 2, 16, LANES), BF16),
            pltpu.SemaphoreType.DMA((2, 8)),
            pltpu.SemaphoreType.DMA((2, 8)),
            pltpu.SemaphoreType.DMA((2, copies)),
            pltpu.SemaphoreType.DMA((2, copies)),
            pltpu.SemaphoreType.DMA((2, copies)),
            pltpu.SemaphoreType.DMA((2, copies)),
            pltpu.SemaphoreType.DMA((2,)),
        ],
        compiler_params=pltpu.CompilerParams(
            collective_id=0, has_side_effects=True, vmem_limit_bytes=48 * 1024 * 1024
        ),
    )(
        brick_slot,
        fields,
        weight_one,
        weight_two,
        gain.reshape(1, channels),
        bias.reshape(1, channels),
    )

    def pack(values):
        return values.astype(BF16).reshape(features.shape)

    return (
        pack(out),
        pack(grad_features),
        gw_one,
        gw_two,
        gg.reshape(channels),
        gb.reshape(channels),
    )


def solution(mesh):
    in_specs = (
        P("gx", "gy", None, None),
        P("gx", "gy", None, None),
        P("gx", "gy", None, None, None),
        P(),
        P(),
        P(),
        P(),
    )
    out_specs = (P("gx", "gy", None, None), P("gx", "gy", None, None), P(), P(), P(), P())
    return jax.shard_map(body, mesh=mesh, in_specs=in_specs, out_specs=out_specs, check_vma=False)
```

time: 79.1 us -> 57.6 us (0.73)
  Pallas kernels: 66.5 us -> 46.7 us
  local copies, waits for them, and re-layouts: 11.4 us -> 9.65 us
    pallas_call x1, Pallas kernels: 66.5 us -> 46.7 us  [body(): pl.pallas_call(functools.partial(kernel, size_x, size_y, tiles, scale), o...]
    slice x2 -> x0, local copies, waits for them, and re-layouts: 0.99 us -> none  [pack(): return values[:, :, :4, :channels].astype(BF16).reshape(features.shape)]
    reshape x3 -> x2, local copies, waits for them, and re-layouts: 2.38 us -> 1.55 us  [pack(): return values.astype(BF16).reshape(features.shape)]
where the time goes in v2:
time: 57.6 us; the launch traced here: 57.4 us
  Pallas kernels  46.7 us (81%)
  local copies, waits for them, and re-layouts  9.65 us (17%)
  between operations  0.7 us (1%)
    pallas_call x1, Pallas kernels, body(): pl.pallas_call(functools.partial(kernel, size_x, size_y, tiles, scale), o...  46.7 us
    unnamed x14, local copies, waits for them, and re-layouts  6.22 us
    another operation x2, local copies, waits for them, and re-layouts, body(): jnp.stack([features, cotangent]).reshape(2, count_slots, 16, 4, channels)  1.88 us
    reshape x2, local copies, waits for them, and re-layouts, pack(): return values.astype(BF16).reshape(features.shape)  1.55 us

profile of v2, /device:TPU:0, one launch (start us, length us, event | category | flops | bytes accessed | tf_op | source)
XLA Modules:
  0.0 57.4 jit_solution(8617242077567677328)
XLA Ops:
  0.6 0.0 copy-start
  0.6 1.0 %stack.9 = bf16[1,4,16,4,96]{4,3,2,1,0:T(4,128)(2,1)S(1)} reshape(bf16[1,1,4,6144]{3,2,1,0:T(4,128)(2,1)} %param.7) | data formatting | bytes 98304 | tf_op jit(solution)/shard_map/stack | solution.py:391
  1.6 0.9 %stack.10 = bf16[1,4,16,4,96]{4,3,2,1,0:T(4,128)(2,1)S(1)} reshape(bf16[1,1,4,6144]{3,2,1,0:T(4,128)(2,1)} %param.8) | data formatting | bytes 98304 | tf_op jit(solution)/shard_map/stack | solution.py:391
  2.5 0.2 fusion.6.fields
  2.8 0.0 copy-done
  2.8 0.0 copy-start.1
  2.8 1.1 %copy-done.1 = bf16[27,96,96]{2,1,0:T(8,128)(2,1)S(1)} copy-done((bf16[27,96,96]{2,1,0:T(8,128)(2,1)S(1)}, bf16[27,96,96]{2,1,0:T(8,128)(2,1)}, u32[]{:S(2)}) %copy-start.1) | copy-done | bytes 497688
  3.9 0.0 copy-start.2
  3.9 0.7 %copy-done.2 = s32[1,1,2,2,2]{4,3,2,1,0:T(2,128)S(1)} copy-done((s32[1,1,2,2,2]{4,3,2,1,0:T(2,128)S(1)}, s32[1,1,2,2,2]{4,3,2,1,0:T(2,128)}, u32[]{:S(2)}) %copy-start.2) | copy-done | bytes 56
  4.5 0.0 copy-start.3
  4.5 0.7 %copy-done.3 = f32[96]{0:T(128)S(1)} copy-done((f32[96]{0:T(128)S(1)}, f32[96]{0:T(128)}, u32[]{:S(2)}) %copy-start.3) | copy-done | bytes 408
  5.2 0.0 copy-start.4
  5.2 0.7 %copy-done.4 = f32[96]{0:T(128)S(1)} copy-done((f32[96]{0:T(128)S(1)}, f32[96]{0:T(128)}, u32[]{:S(2)}) %copy-start.4) | copy-done | bytes 408
  5.9 46.7 %shard_map.118 = (f32[4,16,4,96]{3,2,1,0:T(4,128)S(1)}, f32[4,16,4,96]{3,2,1,0:T(4,128)S(1)}, f32[27,96,96]{2,1,0:T(8,128)S(1)}, f32[27,96,96]{2,1,0:T(8,128)S(1...) custom-call(s32[1,1,2,2,2]{4,3,2,1,0:T(2,128)S(1)} %copy-done.2, f32[2,4,16,8,128]{4,3,2,1,0:T(8,128)S(1)} %fusion.6.fields, ...), custom_call_target="tpu_custom_call" | custom-call | tf_op jit(solution)/shard_map/pallas_call | solution.py:400
  52.6 0.8 %reshape.37 = bf16[1,1,4,6144]{3,2,1,0:T(4,128)(2,1)} reshape(bf16[4,16,4,96]{3,2,1,0:T(4,128)(2,1)S(1)} %convert_element_type.9) | data formatting | bytes 98304 | tf_op jit(solution)/shard_map/reshape | solution.py:445
  53.4 0.8 %reshape.38 = bf16[1,1,4,6144]{3,2,1,0:T(4,128)(2,1)} reshape(bf16[4,16,4,96]{3,2,1,0:T(4,128)(2,1)S(1)} %convert_element_type.10) | data formatting | bytes 98304 | tf_op jit(solution)/shard_map/reshape | solution.py:445
  54.2 1.1 %copy.17 = f32[27,96,96]{2,1,0:T(8,128)} copy(f32[27,96,96]{2,1,0:T(8,128)S(1)} %get-tuple-element.26) | data formatting | bytes 1990656
  55.3 1.1 %copy.18 = f32[27,96,96]{2,1,0:T(8,128)} copy(f32[27,96,96]{2,1,0:T(8,128)S(1)} %get-tuple-element.27) | data formatting | bytes 1990656
  56.3 0.5 copy.19
  56.8 0.5 copy.20
  (2 shorter events, 0.0 us)
Async XLA Ops:
  0.6 2.1 %copy-start = (bf16[27,96,96]{2,1,0:T(8,128)(2,1)S(1)}, bf16[27,96,96]{2,1,0:T(8,128)(2,1)}, u32[]{:S(2)}) copy-start(bf16[27,96,96]{2,1,0:T(8,128)(2,1)} %w_one.1) | copy-start | bytes 1492996
  2.8 1.1 %copy-start.1 = (bf16[27,96,96]{2,1,0:T(8,128)(2,1)S(1)}, bf16[27,96,96]{2,1,0:T(8,128)(2,1)}, u32[]{:S(2)}) copy-start(bf16[27,96,96]{2,1,0:T(8,128)(2,1)} %w_two.1) | copy-start | bytes 1492996
  3.9 0.7 %copy-start.2 = (s32[1,1,2,2,2]{4,3,2,1,0:T(2,128)S(1)}, s32[1,1,2,2,2]{4,3,2,1,0:T(2,128)}, u32[]{:S(2)}) copy-start(s32[1,1,2,2,2]{4,3,2,1,0:T(2,128)} %slots.1) | copy-start | bytes 100
  4.5 0.7 %copy-start.3 = (f32[96]{0:T(128)S(1)}, f32[96]{0:T(128)}, u32[]{:S(2)}) copy-start(f32[96]{0:T(128)} %param.12) | copy-start | bytes 1156
  5.2 0.7 %copy-start.4 = (f32[96]{0:T(128)S(1)}, f32[96]{0:T(128)}, u32[]{:S(2)}) copy-start(f32[96]{0:T(128)} %param.13) | copy-start | bytes 1156

commit v3 on v2

--- a/solution.py
+++ b/solution.py
@@ -44,7 +44,7 @@
     slots, fields, w_one, w_two, gain_in, bias_in,
     out, grad_out, gw_one, gw_two, gg_out, gb_out,
     held, held_two, shifted, cols_a, cols_b, wm_one, wm_two, wt_one, wt_two, pad_rows,
-    raw, w_here, red_a, red_b, in_a, in_b, all_a, all_b,
+    raw, w_here, red_a, red_b, in_a, in_b, wire_a, wire_b, land_a, land_b, all_a, all_b,
     halo_send, halo_recv, sum_send, sum_recv, all_send, all_recv, w_sem,
 ):
     px, py = lax.axis_index("gx"), lax.axis_index("gy")
@@ -163,23 +163,37 @@
     halo_start(held, 0)
 
     raw[...] = jnp.zeros_like(raw)
-    for n, (wide, turned) in enumerate(((wm_one, wt_one), (wm_two, wt_two))):
+
+    def load_raw(n):
         loads[n].wait()
         for t in range(TAPS):
-            raw[t * LANES : t * LANES + 96, 0:96] = w_here[n, t]
+            raw[n, t * LANES : t * LANES + 96, 0:96] = w_here[n, t]
+
+    def widen(n, wide):
+        for block, t in enumerate(HOSTS):
+            at = block * LANES
+            wide[at : at + LANES, :] = raw[n, t * LANES : (t + 1) * LANES, :]
+            if rider(block):
+                extra, third = rider(block)
+                rows = extra * LANES + third * 32
+                wide[at + 96 : at + LANES, :] = raw[n, rows : rows + 32, :]
+
+    def flip(n, turned):
         turns = {}
         for t in range(TAPS):
-            flip = (TAPS - 1 - t) * LANES
-            turns[t] = raw[flip : flip + LANES, :].astype(F32).T.astype(BF16)
+            rows = (TAPS - 1 - t) * LANES
+            turns[t] = raw[n, rows : rows + LANES, :].astype(F32).T.astype(BF16)
         for block, t in enumerate(HOSTS):
             at = block * LANES
-            wide[at : at + LANES, :] = raw[t * LANES : (t + 1) * LANES, :]
             turned[at : at + LANES, :] = turns[t]
             if rider(block):
                 extra, third = rider(block)
-                rows = extra * LANES + third * 32
-                wide[at + 96 : at + LANES, :] = raw[rows : rows + 32, :]
                 turned[at + 96 : at + LANES, :] = turns[extra][third * 32 : third * 32 + 32]
+
+    load_raw(0)
+    widen(0, wm_one)
+    load_raw(1)
+    flip(1, wt_two)
     pad_rows[...] = jnp.zeros_like(pad_rows)
     pad_rows[0:1, 0:96] = gain_in[...]
     pad_rows[1:2, 0:96] = bias_in[...]
@@ -252,9 +266,11 @@
     red_b[BLOCKS * 12, 1:2, :] = jnp.sum(back_pre, axis=0, keepdims=True)
 
     reds, ins, alls = (red_a, red_b), (in_a, in_b), (all_a, all_b)
+    wires, lands = (wire_a, wire_b), (land_a, land_b)
     offsets = ([jnp.int32(0)], [jnp.int32(0)])
     pieces, landings, first_sem = [], [], []
     length, landing, sems = tiles, 0, 0
+    narrow = [stage > 0 and group[1] > 1 for stage, group in enumerate(groups)]
     for group in groups:
         length = length // group[2]
         pieces.append(length)
@@ -269,10 +285,17 @@
         for turn in range(1, group[2]):
             other = lax.rem(rank_in(group) + turn, group[2])
             sem = first_sem[stage] + turn - 1
+            if narrow[stage]:
+                half = piece // 2
+                source = wires[which].at[pl.ds(other * half, half)]
+                target = lands[which].at[pl.ds((turn - 1) * half, half)]
+            else:
+                source = reds[which].at[pl.ds(offsets[which][stage] + other * piece, piece)]
+                target = ins[which].at[pl.ds(landings[stage] + (turn - 1) * piece, piece)]
             copies.append(
                 pltpu.make_async_remote_copy(
-                    src_ref=reds[which].at[pl.ds(offsets[which][stage] + other * piece, piece)],
-                    dst_ref=ins[which].at[pl.ds(landings[stage] + (turn - 1) * piece, piece)],
+                    src_ref=source,
+                    dst_ref=target,
                     send_sem=sum_send.at[which, sem],
                     recv_sem=sum_recv.at[which, sem],
                     device_id=member(group, other),
@@ -308,13 +331,27 @@
         offsets[which].append(keep)
         total = reds[which][pl.ds(keep, piece)]
         for turn in range(group[2] - 1):
-            total = total + ins[which][pl.ds(landings[stage] + turn * piece, piece)]
-        if stage == stages - 1:
-            alls[which][pl.ds(keep // 2, piece // 2)] = (
-                (total * scale).reshape(piece // 2, 16, LANES).astype(BF16)
-            )
-        else:
+            if narrow[stage]:
+                half = piece // 2
+                came = lands[which][pl.ds(turn * half, half)].astype(F32)
+                total = total + came.reshape(piece, 8, LANES)
+            else:
+                total = total + ins[which][pl.ds(landings[stage] + turn * piece, piece)]
+        if stage < stages - 1:
             reds[which][pl.ds(keep, piece)] = total
+            if narrow[stage + 1]:
+                wires[which][...] = total.reshape(piece // 2, 16, LANES).astype(BF16)
+            return
+        total = total * scale
+        if which == 1:
+            rest = total - total.astype(BF16).astype(F32)
+            tile = lax.broadcasted_iota(jnp.int32, total.shape, 0) + keep
+            row = lax.broadcasted_iota(jnp.int32, total.shape, 1)
+            mine = jnp.logical_and(tile == BLOCKS * 12, jnp.logical_and(row >= 2, row < 4))
+            total = jnp.where(mine, pltpu.roll(rest, 2, 1), total)
+        alls[which][pl.ds(keep // 2, piece // 2)] = total.reshape(
+            piece // 2, 16, LANES
+        ).astype(BF16)
 
     def advance(which, step):
         if step > 2 * stages:
@@ -334,12 +371,14 @@
         for copy in copies:
             copy.start()
 
+    weight_sums(interior(held_two, 1), cols_a, red_b)
+    advance(1, 0)
     weight_sums(interior(held_two, 0), cols_b, red_a)
     advance(0, 0)
+    flip(0, wt_one)
+    advance(1, 1)
     halo_arrive(held_two, 1)
     columns(held_two, 1, cols_a)
-    weight_sums(interior(held, 0), cols_a, red_b)
-    advance(1, 0)
     advance(0, 1)
 
     def to_slots(dense, ref):
@@ -354,26 +393,33 @@
             ref[s] = (total + pltpu.roll(total, 4, 1))[:, 0:4, 0:96]
 
     to_slots(interior(held, 1) + dot(cols_a[...], wt_one[...]), grad_out)
-    advance(1, 1)
+    advance(1, 2)
+    widen(1, wm_two)
     columns(held_two, 0, cols_b)
+    advance(1, 3)
     advance(0, 2)
     to_slots(interior(held, 0) + dot(cols_b[...], wm_two[...]), out)
-    def unpack(summed, gw):
-        for block, t in enumerate(HOSTS):
-            values = summed[pl.ds(block * 6, 6)].astype(F32).reshape(96, LANES)
-            gw[TAPS - 1 - t] = values[:, 0:96]
-            if rider(block):
-                extra, third = rider(block)
-                lanes = slice(third * 32, third * 32 + 32)
-                gw[TAPS - 1 - extra, :, lanes] = pltpu.roll(values, third * 32 + 32, 1)[:, lanes]
-
-    for step in range(2, 2 * stages + 1):
+    advance(1, 4)
+    advance(0, 3)
+    for step in range(5, 2 * stages + 1):
         advance(1, step)
-        advance(0, step + 1)
-        if step + 1 == 2 * stages:
-            unpack(all_a, gw_two)
-    unpack(all_b, gw_one)
+        advance(0, step - 1)
+    for block, t in enumerate(HOSTS):
+        values = all_b[pl.ds(block * 6, 6)].astype(F32).reshape(96, LANES).T
+        gw_one[t] = values[0:96, :]
+        if rider(block):
+            extra, third = rider(block)
+            gw_one[extra, third * 32 : third * 32 + 32, :] = values[96:LANES, :]
     last = all_b[BLOCKS * 6].astype(F32)
+    last = last + pltpu.roll(last, 14, 0)
+    advance(0, 2 * stages)
+    for block, t in enumerate(HOSTS):
+        values = all_a[pl.ds(block * 6, 6)].astype(F32).reshape(96, LANES)
+        gw_two[TAPS - 1 - t] = values[:, 0:96]
+        if rider(block):
+            extra, third = rider(block)
+            lanes = slice(third * 32, third * 32 + 32)
+            gw_two[TAPS - 1 - extra, :, lanes] = pltpu.roll(values, third * 32 + 32, 1)[:, lanes]
     gg_out[...] = last[0:1, 0:96]
     gb_out[...] = last[1:2, 0:96]
     halo_sent(held, 0)
@@ -413,12 +459,16 @@
             pltpu.VMEM((BLOCKS * LANES, LANES), BF16),
             pltpu.VMEM((BLOCKS * LANES, LANES), BF16),
             pltpu.VMEM((8, LANES), F32),
-            pltpu.VMEM((TAPS * LANES, LANES), BF16),
+            pltpu.VMEM((2, TAPS * LANES, LANES), BF16),
             pltpu.VMEM((2, TAPS, channels, channels), BF16),
             pltpu.VMEM((tiles, 8, LANES), F32),
             pltpu.VMEM((tiles, 8, LANES), F32),
             pltpu.VMEM((tiles, 8, LANES), F32),
             pltpu.VMEM((tiles, 8, LANES), F32),
+            pltpu.VMEM((tiles // 4, 16, LANES), BF16),
+            pltpu.VMEM((tiles // 4, 16, LANES), BF16),
+            pltpu.VMEM((tiles // 4, 16, LANES), BF16),
+            pltpu.VMEM((tiles // 4, 16, LANES), BF16),
             pltpu.VMEM((tiles // 2, 16, LANES), BF16),
             pltpu.VMEM((tiles // 2, 16, LANES), BF16),
             pltpu.SemaphoreType.DMA((2, 8)),
@@ -430,7 +480,7 @@
             pltpu.SemaphoreType.DMA((2,)),
         ],
         compiler_params=pltpu.CompilerParams(
-            collective_id=0, has_side_effects=True, vmem_limit_bytes=48 * 1024 * 1024
+            collective_id=0, has_side_effects=True, vmem_limit_bytes=62 * 1024 * 1024
         ),
     )(
         brick_slot,

time: 57.6 us -> 54.4 us (0.944)
  Pallas kernels: 46.7 us -> 42.6 us
  other arithmetic: 0.26 us -> 2.86 us
  local copies, waits for them, and re-layouts: 9.65 us -> 8.03 us
    pallas_call x1, Pallas kernels: 46.7 us -> 42.6 us  [body(): pl.pallas_call(functools.partial(kernel, size_x, size_y, tiles, scale), o...]
    convert_element_type x2, other arithmetic: 0.05 us -> 1.86 us  [pack(): return values.astype(BF16).reshape(features.shape)]
    unnamed x14 -> x10, local copies, waits for them, and re-layouts: 6.22 us -> 4.67 us
    pad x1, other arithmetic: 0.21 us -> 1 us  [body(): jnp.pad(fields, ((0, 0), (0, 0), (0, 0), (0, 0), (0, LANES - channels)))]
where the time goes in v3:
time: 54.4 us; the launch traced here: 54.1 us
  Pallas kernels  42.6 us (78%)
  local copies, waits for them, and re-layouts  8.03 us (15%)
  other arithmetic  2.86 us (5%)
  between operations  0.66 us (1%)
    pallas_call x1, Pallas kernels, body(): pl.pallas_call(functools.partial(kernel, size_x, size_y, tiles, scale), o...  42.6 us
    unnamed x10, local copies, waits for them, and re-layouts  4.67 us
    convert_element_type x2, other arithmetic, pack(): return values.astype(BF16).reshape(features.shape)  1.86 us
    another operation x2, local copies, waits for them, and re-layouts, body(): jnp.stack([features, cotangent]).reshape(2, count_slots, 16, 4, channels)  1.82 us
    reshape x2, local copies, waits for them, and re-layouts, pack(): return values.astype(BF16).reshape(features.shape)  1.55 us

profile of v3, /device:TPU:0, one launch (start us, length us, event | category | flops | bytes accessed | tf_op | source)
XLA Modules:
  0.0 54.1 jit_solution(4483825916034111008)
XLA Ops:
  0.6 0.9 %stack.9 = bf16[1,4,16,4,96]{4,3,2,1,0:T(4,128)(2,1)S(1)} reshape(bf16[1,1,4,6144]{3,2,1,0:T(4,128)(2,1)} %param.7) | data formatting | bytes 98304 | tf_op jit(solution)/shard_map/stack | solution.py:437
  1.5 0.9 %stack.10 = bf16[1,4,16,4,96]{4,3,2,1,0:T(4,128)(2,1)S(1)} reshape(bf16[1,1,4,6144]{3,2,1,0:T(4,128)(2,1)} %param.8) | data formatting | bytes 98304 | tf_op jit(solution)/shard_map/stack | solution.py:437
  2.5 1.0 %fusion.6.fields = f32[2,4,16,8,128]{4,3,2,1,0:T(8,128)} fusion(bf16[1,4,16,4,96]{4,3,2,1,0:T(4,128)(2,1)S(1)} %stack.10, bf16[1,4,16,4,96]{4,3,2,1,0:T(4,128)(2,1)S(1)} %stack.9), kind=kLoop, calls=%fused_computation.7 | loop fusion | flops 1703936 | bytes 622592 | tf_op jit(solution)/shard_map/jit(_pad)/pad | solution.py:439
  3.5 42.6 %shard_map.118 = (f32[4,16,4,96]{3,2,1,0:T(4,128)}, f32[4,16,4,96]{3,2,1,0:T(4,128)}, f32[27,96,96]{2,1,0:T(8,128)}, f32[27,96,96]{2,1,0:T(8,128)}, f32[1,96]{1,0:T(1,128)}, /*index=5*/f32[1,96]{1,0:T(1,128)}) custom-call(s32[1,1,2,2,2]{4,3,2,1,0:T(2,128)} %slots.1, f32[2,4,16,8,128]{4,3,2,1,0:T(8,128)} %fusion.6.fields, bf16[27,96,96]{2,1,0:T(8,128)(2,1)} %w_one.1, ...), custom_call_target="tpu_custom_call" | custom-call | tf_op jit(solution)/shard_map/pallas_call | solution.py:446
  46.0 0.9 %convert_element_type.9 = bf16[4,16,4,96]{3,2,1,0:T(4,128)(2,1)S(1)} convert(f32[4,16,4,96]{3,2,1,0:T(4,128)} %get-tuple-element.12) | non-fusion elementwise | flops 24576 | bytes 147456 | tf_op jit(solution)/shard_map/convert_element_type | solution.py:495
  47.0 0.8 %reshape.37 = bf16[1,1,4,6144]{3,2,1,0:T(4,128)(2,1)} reshape(bf16[4,16,4,96]{3,2,1,0:T(4,128)(2,1)S(1)} %convert_element_type.9) | data formatting | bytes 98304 | tf_op jit(solution)/shard_map/reshape | solution.py:495
  47.7 0.9 %convert_element_type.10 = bf16[4,16,4,96]{3,2,1,0:T(4,128)(2,1)S(1)} convert(f32[4,16,4,96]{3,2,1,0:T(4,128)} %get-tuple-element.13) | non-fusion elementwise | flops 24576 | bytes 147456 | tf_op jit(solution)/shard_map/convert_element_type | solution.py:495
  48.7 0.8 %reshape.38 = bf16[1,1,4,6144]{3,2,1,0:T(4,128)(2,1)} reshape(bf16[4,16,4,96]{3,2,1,0:T(4,128)(2,1)S(1)} %convert_element_type.10) | data formatting | bytes 98304 | tf_op jit(solution)/shard_map/reshape | solution.py:495
  49.4 0.0 copy-start
  49.4 2.6 %copy.17 = f32[27,96,96]{2,1,0:T(8,128)} copy(f32[27,96,96]{2,1,0:T(8,128)} %get-tuple-element.26) | data formatting | bytes 1990656
  52.0 0.0 copy-done
  52.0 0.0 copy-start.2
  52.0 0.0 copy-start.1
  52.0 1.1 %copy.18 = f32[27,96,96]{2,1,0:T(8,128)} copy(f32[27,96,96]{2,1,0:T(8,128)S(1)} %copy-done) | data formatting | bytes 1990656
  53.1 0.0 copy-done.2
  53.1 0.5 copy.19
  53.6 0.0 copy-done.1
  53.6 0.5 copy.20
Async XLA Ops:
  49.4 2.6 %copy-start = (f32[27,96,96]{2,1,0:T(8,128)S(1)}, f32[27,96,96]{2,1,0:T(8,128)}, u32[]{:S(2)}) copy-start(f32[27,96,96]{2,1,0:T(8,128)} %get-tuple-element.27) | copy-start | bytes 2985988
  52.0 1.1 %copy-start.2 = (f32[1,96]{1,0:T(1,128)S(1)}, f32[1,96]{1,0:T(1,128)}, u32[]{:S(2)}) copy-start(f32[1,96]{1,0:T(1,128)} %get-tuple-element.16) | copy-start | bytes 1156
  52.0 1.6 %copy-start.1 = (f32[1,96]{1,0:T(1,128)S(1)}, f32[1,96]{1,0:T(1,128)}, u32[]{:S(2)}) copy-start(f32[1,96]{1,0:T(1,128)} %get-tuple-element.17) | copy-start | bytes 1156

commit v4 on v3

--- a/solution.py
+++ b/solution.py
@@ -25,13 +25,16 @@
     return pl.ds(1, 8) if step == 0 else pl.ds(0 if step > 0 else 9, 1)
 
 
-RIDERS = (1, 4, 7, 10, 13, 16)
-HOSTS = tuple(t for t in range(TAPS) if t not in RIDERS)
+PLANE_RIDERS = (1, 4)
+PLANE_HOSTS = (0, 2, 3, 5, 6, 7, 8)
+PLANE = len(PLANE_HOSTS)
+HOSTS = tuple(9 * a + u for a in range(3) for u in PLANE_HOSTS)
 BLOCKS = len(HOSTS)
 
 
 def rider(block):
-    return (RIDERS[block // 3], block % 3) if block < 3 * len(RIDERS) else None
+    a, n = divmod(block, PLANE)
+    return (9 * a + PLANE_RIDERS[n // 3], n % 3) if n < 6 else None
 
 
 def sum_groups(size_x, size_y):
@@ -41,9 +44,9 @@
 
 def kernel(
     size_x, size_y, tiles, scale,
-    slots, fields, w_one, w_two, gain_in, bias_in,
+    small, fields, w_one, w_two,
     out, grad_out, gw_one, gw_two, gg_out, gb_out,
-    held, held_two, shifted, cols_a, cols_b, wm_one, wm_two, wt_one, wt_two, pad_rows,
+    held, held_two, shifted, cols_a, cols_b, wm_one, wm_two, wt_one, wt_two,
     raw, w_here, red_a, red_b, in_a, in_b, wire_a, wire_b, land_a, land_b, all_a, all_b,
     halo_send, halo_recv, sum_send, sum_recv, all_send, all_recv, w_sem,
 ):
@@ -102,12 +105,12 @@
     lane_index = lax.broadcasted_iota(jnp.int32, (1, 8, LANES), 2)
     low_half = jnp.where(z_index < 4, 1.0, 0.0).astype(F32)
     high_half = 1.0 - low_half
-    cell_slot = [slots[0, 0, c // 4, c // 2 % 2, c % 2] for c in range(8)]
+    cell_slot = [small[8 + c : 9 + c, :].reshape(1, 1, LANES) for c in range(8)]
 
     def picks(i, j, s):
         cell = (i * 2 + j) * 2
-        lower = jnp.where(cell_slot[cell] == s, 1.0, 0.0).astype(F32)
-        upper = jnp.where(cell_slot[cell + 1] == s, 1.0, 0.0).astype(F32)
+        lower = 1.0 - jnp.minimum(jnp.abs(cell_slot[cell] - s), 1.0)
+        upper = 1.0 - jnp.minimum(jnp.abs(cell_slot[cell + 1] - s), 1.0)
         return lower * low_half + upper * high_half
 
     masks = {(i, j, s): picks(i, j, s) for i in range(2) for j in range(2) for s in range(4)}
@@ -194,11 +197,8 @@
     widen(0, wm_one)
     load_raw(1)
     flip(1, wt_two)
-    pad_rows[...] = jnp.zeros_like(pad_rows)
-    pad_rows[0:1, 0:96] = gain_in[...]
-    pad_rows[1:2, 0:96] = bias_in[...]
-    gain = pad_rows[0:1, :]
-    bias = pad_rows[1:2, :]
+    gain = small[0:1, :]
+    bias = small[1:2, :]
     red_a[...] = jnp.zeros_like(red_a)
     red_b[...] = jnp.zeros_like(red_b)
 
@@ -217,12 +217,12 @@
                 10, 10, 8, LANES
             )
 
-        def window(t, version):
-            a, b = t // 9, t // 3 % 3
-            return shifted[version, a : a + 8, b : b + 8].reshape(512, LANES)
-
-        for block, t in enumerate(HOSTS):
-            values = window(t, t % 3)
+        def window(u, version):
+            b = u // 3 % 3
+            return shifted[version, :, b : b + 8].reshape(640, LANES)
+
+        for block, u in enumerate(PLANE_HOSTS):
+            values = window(u, u % 3)
             if rider(block):
                 values = values + window(rider(block)[0], 3 + rider(block)[1])
             cols[:, block * LANES : (block + 1) * LANES] = values.astype(BF16)
@@ -242,23 +242,37 @@
     def dot(lhs, rhs):
         return jnp.dot(lhs, rhs, preferred_element_type=F32)
 
+    def conv(cols, wide):
+        total = None
+        for a in range(3):
+            part = dot(
+                cols[64 * a : 64 * a + 512, :],
+                wide[a * PLANE * LANES : (a + 1) * PLANE * LANES, :],
+            )
+            total = part if total is None else total + part
+        return total
+
     def weight_sums(left, cols, red):
         left_t = left.T.astype(BF16)[0:96]
-        for block in range(BLOCKS):
-            red[pl.ds(block * 12, 12)] = dot(
-                left_t, cols[:, block * LANES : (block + 1) * LANES]
-            ).reshape(12, 8, LANES)
+        for a in range(3):
+            for n in range(0, PLANE, 2):
+                last = min(n + 2, PLANE)
+                product = dot(left_t, cols[64 * a : 64 * a + 512, n * LANES : last * LANES])
+                for k in range(last - n):
+                    red[pl.ds((a * PLANE + n + k) * 12, 12)] = product[
+                        :, k * LANES : (k + 1) * LANES
+                    ].reshape(12, 8, LANES)
 
     halo_arrive(held, 0)
     occupied = dense_mask()
     columns(held, 0, cols_a)
-    first_conv = dot(cols_a[...], wm_one[...]) * occupied
+    first_conv = conv(cols_a, wm_one) * occupied
     pre = first_conv * gain + bias
     sigmoid = 1.0 / (1.0 + jnp.exp(-pre))
     hidden = occupied * (pre * sigmoid)
     held_two[0, 1:9, 1:9] = hidden.reshape(8, 8, 8, LANES)
     columns(held, 1, cols_b)
-    back_hidden = dot(cols_b[...], wt_two[...]) * occupied
+    back_hidden = conv(cols_b, wt_two) * occupied
     back_pre = back_hidden * (sigmoid * (1.0 + pre * (1.0 - sigmoid)))
     held_two[1, 1:9, 1:9] = (back_pre * gain).reshape(8, 8, 8, LANES)
     halo_start(held_two, 1)
@@ -392,15 +406,17 @@
                     total = part if total is None else total + part
             ref[s] = (total + pltpu.roll(total, 4, 1))[:, 0:4, 0:96]
 
-    to_slots(interior(held, 1) + dot(cols_a[...], wt_one[...]), grad_out)
+    back_inputs = conv(cols_a, wt_one)
     advance(1, 2)
+    to_slots(interior(held, 1) + back_inputs, grad_out)
+    advance(0, 2)
     widen(1, wm_two)
     columns(held_two, 0, cols_b)
     advance(1, 3)
-    advance(0, 2)
-    to_slots(interior(held, 0) + dot(cols_b[...], wm_two[...]), out)
+    second_conv = conv(cols_b, wm_two)
+    advance(0, 3)
     advance(1, 4)
-    advance(0, 3)
+    to_slots(interior(held, 0) + second_conv, out)
     for step in range(5, 2 * stages + 1):
         advance(1, step)
         advance(0, step - 1)
@@ -437,8 +453,16 @@
     fields = jnp.stack([features, cotangent]).reshape(2, count_slots, 16, 4, channels)
     fields = jnp.concatenate([fields, fields], axis=3).astype(F32)
     fields = jnp.pad(fields, ((0, 0), (0, 0), (0, 0), (0, 0), (0, LANES - channels)))
+    spare = ((0, 0), (0, LANES - channels))
+    small = jnp.concatenate(
+        [
+            jnp.pad(gain.reshape(1, channels), spare),
+            jnp.pad(bias.reshape(1, channels), spare),
+            jnp.zeros((6, LANES), F32),
+            jnp.broadcast_to(brick_slot.reshape(8, 1).astype(F32), (8, LANES)),
+        ]
+    )
     vmem = pl.BlockSpec(memory_space=pltpu.VMEM)
-    smem = pl.BlockSpec(memory_space=pltpu.SMEM)
     hbm = pl.BlockSpec(memory_space=pltpu.HBM)
     slot_shape = jax.ShapeDtypeStruct((count_slots, 16, 4, channels), F32)
     weight_shape = jax.ShapeDtypeStruct((TAPS, channels, channels), F32)
@@ -446,19 +470,18 @@
     out, grad_features, gw_one, gw_two, gg, gb = pl.pallas_call(
         functools.partial(kernel, size_x, size_y, tiles, scale),
         out_shape=(slot_shape, slot_shape, weight_shape, weight_shape, row_shape, row_shape),
-        in_specs=[smem, vmem, hbm, hbm, vmem, vmem],
+        in_specs=[vmem, vmem, hbm, hbm],
         out_specs=(vmem,) * 6,
         scratch_shapes=[
             pltpu.VMEM((2, 10, 10, 8, LANES), F32),
             pltpu.VMEM((2, 10, 10, 8, LANES), F32),
             pltpu.VMEM((6, 10, 10, 8, LANES), F32),
-            pltpu.VMEM((512, BLOCKS * LANES), BF16),
-            pltpu.VMEM((512, BLOCKS * LANES), BF16),
+            pltpu.VMEM((640, PLANE * LANES), BF16),
+            pltpu.VMEM((640, PLANE * LANES), BF16),
             pltpu.VMEM((BLOCKS * LANES, LANES), BF16),
             pltpu.VMEM((BLOCKS * LANES, LANES), BF16),
             pltpu.VMEM((BLOCKS * LANES, LANES), BF16),
             pltpu.VMEM((BLOCKS * LANES, LANES), BF16),
-            pltpu.VMEM((8, LANES), F32),
             pltpu.VMEM((2, TAPS * LANES, LANES), BF16),
             pltpu.VMEM((2, TAPS, channels, channels), BF16),
             pltpu.VMEM((tiles, 8, LANES), F32),
@@ -480,15 +503,13 @@
             pltpu.SemaphoreType.DMA((2,)),
         ],
         compiler_params=pltpu.CompilerParams(
-            collective_id=0, has_side_effects=True, vmem_limit_bytes=62 * 1024 * 1024
+            collective_id=0, has_side_effects=True, vmem_limit_bytes=48 * 1024 * 1024
         ),
     )(
-        brick_slot,
+        small,
         fields,
         weight_one,
         weight_two,
-        gain.reshape(1, channels),
-        bias.reshape(1, channels),
     )
 
     def pack(values):

time: 54.4 us -> 50.7 us (0.932)
  Pallas kernels: 42.6 us -> 40.1 us
  other arithmetic: 2.86 us -> 1.74 us
    pallas_call x1, Pallas kernels: 42.6 us -> 40.1 us  [body(): pl.pallas_call(functools.partial(kernel, size_x, size_y, tiles, scale), o...]
    convert_element_type x2, other arithmetic: 1.86 us -> 0.05 us  [pack(): return values.astype(BF16).reshape(features.shape)]
    pad x1, other arithmetic: 1 us -> 0.21 us  [body(): jnp.pad(fields, ((0, 0), (0, 0), (0, 0), (0, 0), (0, LANES - channels)))]
    concatenate x0 -> x1, other arithmetic: none -> 0.74 us  [body(): jnp.concatenate([jnp.pad(gain.reshape(1, channels), spare), jnp.pad(bias....]
    convert_element_type x0 -> x1, other arithmetic: none -> 0.73 us  [body(): brick_slot.reshape(8, 1).astype(F32)]
    unnamed x10 -> x8, local copies, waits for them, and re-layouts: 4.67 us -> 4.23 us
where the time goes in v4:
time: 50.7 us; the launch traced here: 50.4 us
  Pallas kernels  40.1 us (79%)
  local copies, waits for them, and re-layouts  7.84 us (15%)
  other arithmetic  1.74 us (3%)
  between operations  0.71 us (1%)
    pallas_call x1, Pallas kernels, body(): pl.pallas_call(functools.partial(kernel, size_x, size_y, tiles, scale), o...  40.1 us
    unnamed x8, local copies, waits for them, and re-layouts  4.23 us
    another operation x2, local copies, waits for them, and re-layouts, body(): jnp.stack([features, cotangent]).reshape(2, count_slots, 16, 4, channels)  1.82 us
    reshape x2, local copies, waits for them, and re-layouts, pack(): return values.astype(BF16).reshape(features.shape)  1.55 us

profile of v4, /device:TPU:0, one launch (start us, length us, event | category | flops | bytes accessed | tf_op | source)
XLA Modules:
  0.0 50.4 jit_solution(16343393966127724722)
XLA Ops:
  0.6 0.0 copy-start
  0.7 0.1 pad.23.clone
  0.7 0.7 %convert_element_type.23 = f32[1,1,2,2,2]{4,3,2,1,0:T(2,128)S(1)} convert(s32[1,1,2,2,2]{4,3,2,1,0:T(2,128)} %param.9) | non-fusion elementwise | flops 8 | bytes 64 | tf_op jit(solution)/shard_map/convert_element_type | solution.py:462
  1.5 0.1 reshape.50
  1.5 0.1 pad.24.clone
  1.6 0.7 %fusion.9.small = f32[16,128]{1,0:T(8,128)S(1)} fusion(f32[1,96]{1,0:T(1,128)} %bitcast.6, f32[1,96]{1,0:T(1,128)} %bitcast.7, f32[16]{0:T(128)S(1)} %pad.24.clone, f32[16]{0:T(128)S(1)} %pad.23.clone), kind=kLoop, calls=%fused_computation.13 | loop fusion | flops 18432 | bytes 9088 | tf_op jit(solution)/shard_map/concatenate | solution.py:457
  2.4 0.9 %stack.9 = bf16[1,4,16,4,96]{4,3,2,1,0:T(4,128)(2,1)S(1)} reshape(bf16[1,1,4,6144]{3,2,1,0:T(4,128)(2,1)} %param.7) | data formatting | bytes 98304 | tf_op jit(solution)/shard_map/stack | solution.py:453
  3.3 0.9 %stack.10 = bf16[1,4,16,4,96]{4,3,2,1,0:T(4,128)(2,1)S(1)} reshape(bf16[1,1,4,6144]{3,2,1,0:T(4,128)(2,1)} %param.8) | data formatting | bytes 98304 | tf_op jit(solution)/shard_map/stack | solution.py:453
  4.2 0.2 fusion.6.fields
  4.4 0.0 copy-done
  4.4 0.0 copy-start.1
  4.4 1.1 %copy-done.1 = bf16[27,96,96]{2,1,0:T(8,128)(2,1)S(1)} copy-done((bf16[27,96,96]{2,1,0:T(8,128)(2,1)S(1)}, bf16[27,96,96]{2,1,0:T(8,128)(2,1)}, u32[]{:S(2)}) %copy-start.1) | copy-done | bytes 497688
  5.5 40.1 %shard_map.118 = (f32[4,16,4,96]{3,2,1,0:T(4,128)S(1)}, f32[4,16,4,96]{3,2,1,0:T(4,128)S(1)}, f32[27,96,96]{2,1,0:T(8,128)S(1)}, f32[27,96,96]{2,1,0:T(8,128)S(1...) custom-call(f32[16,128]{1,0:T(8,128)S(1)} %fusion.9.small, f32[2,4,16,8,128]{4,3,2,1,0:T(8,128)S(1)} %fusion.6.fields, ...), custom_call_target="tpu_custom_call" | custom-call | tf_op jit(solution)/shard_map/pallas_call | solution.py:470
  45.6 0.8 %reshape.46 = bf16[1,1,4,6144]{3,2,1,0:T(4,128)(2,1)} reshape(bf16[4,16,4,96]{3,2,1,0:T(4,128)(2,1)S(1)} %convert_element_type.25) | data formatting | bytes 98304 | tf_op jit(solution)/shard_map/reshape | solution.py:516
  46.4 0.8 %reshape.47 = bf16[1,1,4,6144]{3,2,1,0:T(4,128)(2,1)} reshape(bf16[4,16,4,96]{3,2,1,0:T(4,128)(2,1)S(1)} %convert_element_type.26) | data formatting | bytes 98304 | tf_op jit(solution)/shard_map/reshape | solution.py:516
  47.2 1.1 %copy.17 = f32[27,96,96]{2,1,0:T(8,128)} copy(f32[27,96,96]{2,1,0:T(8,128)S(1)} %get-tuple-element.26) | data formatting | bytes 1990656
  48.3 1.1 %copy.18 = f32[27,96,96]{2,1,0:T(8,128)} copy(f32[27,96,96]{2,1,0:T(8,128)S(1)} %get-tuple-element.27) | data formatting | bytes 1990656
  49.3 0.5 %copy.19 = f32[96]{0:T(128)} copy(f32[96]{0:T(128)S(1)} %bitcast.5) | data formatting | bytes 768
  49.8 0.5 %copy.20 = f32[96]{0:T(128)} copy(f32[96]{0:T(128)S(1)} %bitcast.4) | data formatting | bytes 768
  (3 shorter events, 0.1 us)
Async XLA Ops:
  0.6 3.8 %copy-start = (bf16[27,96,96]{2,1,0:T(8,128)(2,1)S(1)}, bf16[27,96,96]{2,1,0:T(8,128)(2,1)}, u32[]{:S(2)}) copy-start(bf16[27,96,96]{2,1,0:T(8,128)(2,1)} %w_one.1) | copy-start | bytes 1492996
  4.4 1.1 %copy-start.1 = (bf16[27,96,96]{2,1,0:T(8,128)(2,1)S(1)}, bf16[27,96,96]{2,1,0:T(8,128)(2,1)}, u32[]{:S(2)}) copy-start(bf16[27,96,96]{2,1,0:T(8,128)(2,1)} %w_two.1) | copy-start | bytes 1492996

commit v5 on v4

--- a/solution.py
+++ b/solution.py
@@ -262,22 +262,6 @@
                     red[pl.ds((a * PLANE + n + k) * 12, 12)] = product[
                         :, k * LANES : (k + 1) * LANES
                     ].reshape(12, 8, LANES)
-
-    halo_arrive(held, 0)
-    occupied = dense_mask()
-    columns(held, 0, cols_a)
-    first_conv = conv(cols_a, wm_one) * occupied
-    pre = first_conv * gain + bias
-    sigmoid = 1.0 / (1.0 + jnp.exp(-pre))
-    hidden = occupied * (pre * sigmoid)
-    held_two[0, 1:9, 1:9] = hidden.reshape(8, 8, 8, LANES)
-    columns(held, 1, cols_b)
-    back_hidden = conv(cols_b, wt_two) * occupied
-    back_pre = back_hidden * (sigmoid * (1.0 + pre * (1.0 - sigmoid)))
-    held_two[1, 1:9, 1:9] = (back_pre * gain).reshape(8, 8, 8, LANES)
-    halo_start(held_two, 1)
-    red_b[BLOCKS * 12, 0:1, :] = jnp.sum(back_pre * first_conv, axis=0, keepdims=True)
-    red_b[BLOCKS * 12, 1:2, :] = jnp.sum(back_pre, axis=0, keepdims=True)
 
     reds, ins, alls = (red_a, red_b), (in_a, in_b), (all_a, all_b)
     wires, lands = (wire_a, wire_b), (land_a, land_b)
@@ -385,15 +369,32 @@
         for copy in copies:
             copy.start()
 
+    halo_arrive(held, 0)
+    occupied = dense_mask()
+    columns(held, 0, cols_a)
+    first_conv = conv(cols_a, wm_one) * occupied
+    pre = first_conv * gain + bias
+    sigmoid = 1.0 / (1.0 + jnp.exp(-pre))
+    hidden = occupied * (pre * sigmoid)
+    held_two[0, 1:9, 1:9] = hidden.reshape(8, 8, 8, LANES)
+    columns(held, 1, cols_b)
+    weight_sums(hidden, cols_b, red_a)
+    advance(0, 0)
+    back_hidden = conv(cols_b, wt_two) * occupied
+    back_pre = back_hidden * (sigmoid * (1.0 + pre * (1.0 - sigmoid)))
+    held_two[1, 1:9, 1:9] = (back_pre * gain).reshape(8, 8, 8, LANES)
+    halo_start(held_two, 1)
+    red_b[BLOCKS * 12, 0:1, :] = jnp.sum(back_pre * first_conv, axis=0, keepdims=True)
+    red_b[BLOCKS * 12, 1:2, :] = jnp.sum(back_pre, axis=0, keepdims=True)
+
+    advance(0, 1)
     weight_sums(interior(held_two, 1), cols_a, red_b)
     advance(1, 0)
-    weight_sums(interior(held_two, 0), cols_b, red_a)
-    advance(0, 0)
     flip(0, wt_one)
     advance(1, 1)
+    advance(0, 2)
     halo_arrive(held_two, 1)
     columns(held_two, 1, cols_a)
-    advance(0, 1)
 
     def to_slots(dense, ref):
         dense = dense.reshape(8, 8, 8, LANES)
@@ -406,20 +407,27 @@
                     total = part if total is None else total + part
             ref[s] = (total + pltpu.roll(total, 4, 1))[:, 0:4, 0:96]
 
-    back_inputs = conv(cols_a, wt_one)
-    advance(1, 2)
-    to_slots(interior(held, 1) + back_inputs, grad_out)
-    advance(0, 2)
+    to_slots(interior(held, 1) + conv(cols_a, wt_one), grad_out)
     widen(1, wm_two)
     columns(held_two, 0, cols_b)
-    advance(1, 3)
+    advance(1, 2)
     second_conv = conv(cols_b, wm_two)
     advance(0, 3)
+    to_slots(interior(held, 0) + second_conv, out)
+    advance(0, 4)
+    advance(1, 3)
     advance(1, 4)
-    to_slots(interior(held, 0) + second_conv, out)
+    for step in range(5, 2 * stages + 1):
+        advance(0, step)
+    for block, t in enumerate(HOSTS):
+        values = all_a[pl.ds(block * 6, 6)].astype(F32).reshape(96, LANES)
+        gw_two[TAPS - 1 - t] = values[:, 0:96]
+        if rider(block):
+            extra, third = rider(block)
+            lanes = slice(third * 32, third * 32 + 32)
+            gw_two[TAPS - 1 - extra, :, lanes] = pltpu.roll(values, third * 32 + 32, 1)[:, lanes]
     for step in range(5, 2 * stages + 1):
         advance(1, step)
-        advance(0, step - 1)
     for block, t in enumerate(HOSTS):
         values = all_b[pl.ds(block * 6, 6)].astype(F32).reshape(96, LANES).T
         gw_one[t] = values[0:96, :]
@@ -428,14 +436,6 @@
             gw_one[extra, third * 32 : third * 32 + 32, :] = values[96:LANES, :]
     last = all_b[BLOCKS * 6].astype(F32)
     last = last + pltpu.roll(last, 14, 0)
-    advance(0, 2 * stages)
-    for block, t in enumerate(HOSTS):
-        values = all_a[pl.ds(block * 6, 6)].astype(F32).reshape(96, LANES)
-        gw_two[TAPS - 1 - t] = values[:, 0:96]
-        if rider(block):
-            extra, third = rider(block)
-            lanes = slice(third * 32, third * 32 + 32)
-            gw_two[TAPS - 1 - extra, :, lanes] = pltpu.roll(values, third * 32 + 32, 1)[:, lanes]
     gg_out[...] = last[0:1, 0:96]
     gb_out[...] = last[1:2, 0:96]
     halo_sent(held, 0)

time: 50.7 us -> 49.7 us (0.980)
  Pallas kernels: 40.1 us -> 39.1 us
    pallas_call x1, Pallas kernels: 40.1 us -> 39.1 us  [body(): pl.pallas_call(functools.partial(kernel, size_x, size_y, tiles, scale), o...]
where the time goes in v5:
time: 49.7 us; the launch traced here: 49.4 us
  Pallas kernels  39.1 us (79%)
  local copies, waits for them, and re-layouts  7.84 us (16%)
  other arithmetic  1.74 us (4%)
  between operations  0.71 us (1%)
    pallas_call x1, Pallas kernels, body(): pl.pallas_call(functools.partial(kernel, size_x, size_y, tiles, scale), o...  39.1 us
    unnamed x8, local copies, waits for them, and re-layouts  4.23 us
    another operation x2, local copies, waits for them, and re-layouts, body(): jnp.stack([features, cotangent]).reshape(2, count_slots, 16, 4, channels)  1.82 us
    reshape x2, local copies, waits for them, and re-layouts, pack(): return values.astype(BF16).reshape(features.shape)  1.55 us

profile of v5, /device:TPU:0, one launch (start us, length us, event | category | flops | bytes accessed | tf_op | source)
XLA Modules:
  0.0 49.4 jit_solution(5924264028206043038)
XLA Ops:
  0.6 0.0 copy-start
  0.7 0.1 pad.23.clone
  0.7 0.7 %convert_element_type.23 = f32[1,1,2,2,2]{4,3,2,1,0:T(2,128)S(1)} convert(s32[1,1,2,2,2]{4,3,2,1,0:T(2,128)} %param.9) | non-fusion elementwise | flops 8 | bytes 64 | tf_op jit(solution)/shard_map/convert_element_type | solution.py:462
  1.5 0.1 reshape.50
  1.5 0.1 pad.24.clone
  1.6 0.7 %fusion.9.small = f32[16,128]{1,0:T(8,128)S(1)} fusion(f32[1,96]{1,0:T(1,128)} %bitcast.6, f32[1,96]{1,0:T(1,128)} %bitcast.7, f32[16]{0:T(128)S(1)} %pad.24.clone, f32[16]{0:T(128)S(1)} %pad.23.clone), kind=kLoop, calls=%fused_computation.13 | loop fusion | flops 18432 | bytes 9088 | tf_op jit(solution)/shard_map/concatenate | solution.py:457
  2.4 0.9 %stack.9 = bf16[1,4,16,4,96]{4,3,2,1,0:T(4,128)(2,1)S(1)} reshape(bf16[1,1,4,6144]{3,2,1,0:T(4,128)(2,1)} %param.7) | data formatting | bytes 98304 | tf_op jit(solution)/shard_map/stack | solution.py:453
  3.3 0.9 %stack.10 = bf16[1,4,16,4,96]{4,3,2,1,0:T(4,128)(2,1)S(1)} reshape(bf16[1,1,4,6144]{3,2,1,0:T(4,128)(2,1)} %param.8) | data formatting | bytes 98304 | tf_op jit(solution)/shard_map/stack | solution.py:453
  4.2 0.2 fusion.6.fields
  4.4 0.0 copy-done
  4.4 0.0 copy-start.1
  4.4 1.1 %copy-done.1 = bf16[27,96,96]{2,1,0:T(8,128)(2,1)S(1)} copy-done((bf16[27,96,96]{2,1,0:T(8,128)(2,1)S(1)}, bf16[27,96,96]{2,1,0:T(8,128)(2,1)}, u32[]{:S(2)}) %copy-start.1) | copy-done | bytes 497688
  5.5 39.1 %shard_map.118 = (f32[4,16,4,96]{3,2,1,0:T(4,128)S(1)}, f32[4,16,4,96]{3,2,1,0:T(4,128)S(1)}, f32[27,96,96]{2,1,0:T(8,128)S(1)}, f32[27,96,96]{2,1,0:T(8,128)S(1...) custom-call(f32[16,128]{1,0:T(8,128)S(1)} %fusion.9.small, f32[2,4,16,8,128]{4,3,2,1,0:T(8,128)S(1)} %fusion.6.fields, ...), custom_call_target="tpu_custom_call" | custom-call | tf_op jit(solution)/shard_map/pallas_call | solution.py:470
  44.7 0.8 %reshape.46 = bf16[1,1,4,6144]{3,2,1,0:T(4,128)(2,1)} reshape(bf16[4,16,4,96]{3,2,1,0:T(4,128)(2,1)S(1)} %convert_element_type.25) | data formatting | bytes 98304 | tf_op jit(solution)/shard_map/reshape | solution.py:516
  45.5 0.8 %reshape.47 = bf16[1,1,4,6144]{3,2,1,0:T(4,128)(2,1)} reshape(bf16[4,16,4,96]{3,2,1,0:T(4,128)(2,1)S(1)} %convert_element_type.26) | data formatting | bytes 98304 | tf_op jit(solution)/shard_map/reshape | solution.py:516
  46.3 1.1 %copy.17 = f32[27,96,96]{2,1,0:T(8,128)} copy(f32[27,96,96]{2,1,0:T(8,128)S(1)} %get-tuple-element.26) | data formatting | bytes 1990656
  47.3 1.1 %copy.18 = f32[27,96,96]{2,1,0:T(8,128)} copy(f32[27,96,96]{2,1,0:T(8,128)S(1)} %get-tuple-element.27) | data formatting | bytes 1990656
  48.4 0.5 %copy.19 = f32[96]{0:T(128)} copy(f32[96]{0:T(128)S(1)} %bitcast.5) | data formatting | bytes 768
  48.9 0.5 %copy.20 = f32[96]{0:T(128)} copy(f32[96]{0:T(128)S(1)} %bitcast.4) | data formatting | bytes 768
  (3 shorter events, 0.1 us)
Async XLA Ops:
  0.6 3.8 %copy-start = (bf16[27,96,96]{2,1,0:T(8,128)(2,1)S(1)}, bf16[27,96,96]{2,1,0:T(8,128)(2,1)}, u32[]{:S(2)}) copy-start(bf16[27,96,96]{2,1,0:T(8,128)(2,1)} %w_one.1) | copy-start | bytes 1492996
  4.4 1.1 %copy-start.1 = (bf16[27,96,96]{2,1,0:T(8,128)(2,1)S(1)}, bf16[27,96,96]{2,1,0:T(8,128)(2,1)}, u32[]{:S(2)}) copy-start(bf16[27,96,96]{2,1,0:T(8,128)(2,1)} %w_two.1) | copy-start | bytes 1492996

commit v6 on v5

--- a/solution.py
+++ b/solution.py
@@ -320,6 +320,20 @@
                 )
             )
         return copies
+
+    def forward(which, turn):
+        group, piece = groups[1], pieces[1] // 2
+        owner = lax.rem(rank_in(group) + group[2] - turn, group[2])
+        rows = alls[which].at[pl.ds(offsets[which][1] // 2 + owner * piece, piece)]
+        pair = groups[0]
+        return pltpu.make_async_remote_copy(
+            src_ref=rows,
+            dst_ref=rows,
+            send_sem=all_send.at[which, sems + turn],
+            recv_sem=all_recv.at[which, sems + turn],
+            device_id=member(pair, lax.rem(rank_in(pair) + 1, pair[2])),
+            device_id_type=MESH,
+        )
 
     def scatter_end(which, stage):
         group, piece = groups[stage], pieces[stage]
@@ -352,7 +366,14 @@
         ).astype(BF16)
 
     def advance(which, step):
-        if step > 2 * stages:
+        if stages == 3 and step > 4:
+            if step == 5:
+                for number, copy in enumerate(gather_copies(which, 1)):
+                    copy.wait()
+                    forward(which, number + 1).start()
+            else:
+                for turn in range(groups[1][2]):
+                    forward(which, turn).wait()
             return
         if step > 0:
             if step <= stages:
@@ -368,6 +389,8 @@
             copies = []
         for copy in copies:
             copy.start()
+        if stages == 3 and step == 4:
+            forward(which, 0).start()
 
     halo_arrive(held, 0)
     occupied = dense_mask()
@@ -498,8 +521,8 @@
             pltpu.SemaphoreType.DMA((2, 8)),
             pltpu.SemaphoreType.DMA((2, copies)),
             pltpu.SemaphoreType.DMA((2, copies)),
-            pltpu.SemaphoreType.DMA((2, copies)),
-            pltpu.SemaphoreType.DMA((2, copies)),
+            pltpu.SemaphoreType.DMA((2, copies + size_x // 2)),
+            pltpu.SemaphoreType.DMA((2, copies + size_x // 2)),
             pltpu.SemaphoreType.DMA((2,)),
         ],
         compiler_params=pltpu.CompilerParams(

time: 49.7 us -> 49.6 us (level)
  no operation moved by 1% of the time
where the time goes in v6:
time: 49.6 us; the launch traced here: 49.3 us
  Pallas kernels  39 us (79%)
  local copies, waits for them, and re-layouts  7.84 us (16%)
  other arithmetic  1.74 us (4%)
  between operations  0.71 us (1%)
    pallas_call x1, Pallas kernels, body(): pl.pallas_call(functools.partial(kernel, size_x, size_y, tiles, scale), o...  39 us
    unnamed x8, local copies, waits for them, and re-layouts  4.23 us
    another operation x2, local copies, waits for them, and re-layouts, body(): jnp.stack([features, cotangent]).reshape(2, count_slots, 16, 4, channels)  1.82 us
    reshape x2, local copies, waits for them, and re-layouts, pack(): return values.astype(BF16).reshape(features.shape)  1.55 us

profile of v6, /device:TPU:0, one launch (start us, length us, event | category | flops | bytes accessed | tf_op | source)
XLA Modules:
  0.0 49.3 jit_solution(7434209456115548687)
XLA Ops:
  0.6 0.0 copy-start
  0.7 0.1 pad.23.clone
  0.7 0.7 %convert_element_type.23 = f32[1,1,2,2,2]{4,3,2,1,0:T(2,128)S(1)} convert(s32[1,1,2,2,2]{4,3,2,1,0:T(2,128)} %param.9) | non-fusion elementwise | flops 8 | bytes 64 | tf_op jit(solution)/shard_map/convert_element_type | solution.py:485
  1.5 0.1 reshape.50
  1.5 0.1 pad.24.clone
  1.6 0.7 %fusion.9.small = f32[16,128]{1,0:T(8,128)S(1)} fusion(f32[1,96]{1,0:T(1,128)} %bitcast.6, f32[1,96]{1,0:T(1,128)} %bitcast.7, f32[16]{0:T(128)S(1)} %pad.24.clone, f32[16]{0:T(128)S(1)} %pad.23.clone), kind=kLoop, calls=%fused_computation.13 | loop fusion | flops 18432 | bytes 9088 | tf_op jit(solution)/shard_map/concatenate | solution.py:480
  2.4 0.9 %stack.9 = bf16[1,4,16,4,96]{4,3,2,1,0:T(4,128)(2,1)S(1)} reshape(bf16[1,1,4,6144]{3,2,1,0:T(4,128)(2,1)} %param.7) | data formatting | bytes 98304 | tf_op jit(solution)/shard_map/stack | solution.py:476
  3.3 0.9 %stack.10 = bf16[1,4,16,4,96]{4,3,2,1,0:T(4,128)(2,1)S(1)} reshape(bf16[1,1,4,6144]{3,2,1,0:T(4,128)(2,1)} %param.8) | data formatting | bytes 98304 | tf_op jit(solution)/shard_map/stack | solution.py:476
  4.2 0.2 fusion.6.fields
  4.4 0.0 copy-done
  4.4 0.0 copy-start.1
  4.4 1.1 %copy-done.1 = bf16[27,96,96]{2,1,0:T(8,128)(2,1)S(1)} copy-done((bf16[27,96,96]{2,1,0:T(8,128)(2,1)S(1)}, bf16[27,96,96]{2,1,0:T(8,128)(2,1)}, u32[]{:S(2)}) %copy-start.1) | copy-done | bytes 497688
  5.5 39.0 %shard_map.118 = (f32[4,16,4,96]{3,2,1,0:T(4,128)S(1)}, f32[4,16,4,96]{3,2,1,0:T(4,128)S(1)}, f32[27,96,96]{2,1,0:T(8,128)S(1)}, f32[27,96,96]{2,1,0:T(8,128)S(1...) custom-call(f32[16,128]{1,0:T(8,128)S(1)} %fusion.9.small, f32[2,4,16,8,128]{4,3,2,1,0:T(8,128)S(1)} %fusion.6.fields, ...), custom_call_target="tpu_custom_call" | custom-call | tf_op jit(solution)/shard_map/pallas_call | solution.py:493
  44.6 0.8 %reshape.46 = bf16[1,1,4,6144]{3,2,1,0:T(4,128)(2,1)} reshape(bf16[4,16,4,96]{3,2,1,0:T(4,128)(2,1)S(1)} %convert_element_type.25) | data formatting | bytes 98304 | tf_op jit(solution)/shard_map/reshape | solution.py:539
  45.4 0.8 %reshape.47 = bf16[1,1,4,6144]{3,2,1,0:T(4,128)(2,1)} reshape(bf16[4,16,4,96]{3,2,1,0:T(4,128)(2,1)S(1)} %convert_element_type.26) | data formatting | bytes 98304 | tf_op jit(solution)/shard_map/reshape | solution.py:539
  46.2 1.1 %copy.17 = f32[27,96,96]{2,1,0:T(8,128)} copy(f32[27,96,96]{2,1,0:T(8,128)S(1)} %get-tuple-element.26) | data formatting | bytes 1990656
  47.2 1.1 %copy.18 = f32[27,96,96]{2,1,0:T(8,128)} copy(f32[27,96,96]{2,1,0:T(8,128)S(1)} %get-tuple-element.27) | data formatting | bytes 1990656
  48.3 0.5 %copy.19 = f32[96]{0:T(128)} copy(f32[96]{0:T(128)S(1)} %bitcast.5) | data formatting | bytes 768
  48.8 0.5 %copy.20 = f32[96]{0:T(128)} copy(f32[96]{0:T(128)S(1)} %bitcast.4) | data formatting | bytes 768
  (3 shorter events, 0.1 us)
Async XLA Ops:
  0.6 3.8 %copy-start = (bf16[27,96,96]{2,1,0:T(8,128)(2,1)S(1)}, bf16[27,96,96]{2,1,0:T(8,128)(2,1)}, u32[]{:S(2)}) copy-start(bf16[27,96,96]{2,1,0:T(8,128)(2,1)} %w_one.1) | copy-start | bytes 1492996
  4.4 1.1 %copy-start.1 = (bf16[27,96,96]{2,1,0:T(8,128)(2,1)S(1)}, bf16[27,96,96]{2,1,0:T(8,128)(2,1)}, u32[]{:S(2)}) copy-start(bf16[27,96,96]{2,1,0:T(8,128)(2,1)} %w_two.1) | copy-start | bytes 1492996
